TPU v7x, 32 devices: a whole 2x2x4 slice. The times are simulated.
32 devices in a mesh: src: 8 (over y, x, core), tm: 4 (over z).
Axes of the slice: x: 2, y: 2, z: 4, core: 2. Of those that a mesh axis runs over, the one named last changes fastest.
Arguments:
- attitude_design: float32 [4, 131072], P(None, ('src', 'tm')), may hold values from -6 to 6
- source_design: float32 [5, 131072], P(None, ('src', 'tm')), may hold values from -6 to 6
- scan_phase: float32 [131072], P(('src', 'tm')), may hold values from 0 to 1
- obs_weight: float32 [131072], P(('src', 'tm')), may hold values from 0.25 to 4
- obs_residual: float32 [131072], P(('src', 'tm')), may hold values from -6 to 6
- source_id: int32 [131072], P(('src', 'tm')), may hold values from 0 to 2047
- knot_start: int32 [131072], P(('src', 'tm')), may hold values from 0 to 1023
- time_segment: int32 [131072, 1], P(('src', 'tm')), may hold values from 0 to 3; in each aligned block of 4096 rows (0 to 4095, 4096 to 8191, ...) at most 2048 rows name the same one
Outputs:
- source_update: float32 [5, 16384], P(None, 'src')
- attitude_update: float32 [4, 4096], P(None, 'tm')
Inputs may be any that keep to these rules, and one draw needn't show every extreme that they name: `time_segment`: among the observations of one device, at most 2048 fall in any one time segment, and in some device some segment receives exactly 2048.
All inputs are finite; a program needn't handle non-finite values.
Results may differ from a plain program's by a relative error of at most 0.0003.
Values sent between devices are 32-bit elements; how exact they have to be, the bound alone decides.
A program may use at most 64 MiB of HBM per device.

v0:
```python
import jax
import jax.numpy as jnp
from jax import lax
from jax.sharding import PartitionSpec as P

KS = 1024
S_DEV = 2048
ITERS = 4


prior_source = 1.0
prior_attitude = 1.0
index_pairs = [(i, j) for i in range(5) for j in range(i, 5)]
spline_pairs = [(j, d) for d in range(4) for j in range(4 - d)]
component_pairs = [(c, e) for c in range(4) for e in range(c, 4)]


def from_behind(x, axis, by):
    count = lax.axis_size(axis)
    pairs = [(i, i + by) for i in range(count) if 0 <= i + by < count]
    return lax.ppermute(x, axis, pairs)


def with_halo(cells, sides, width):
    for axis, dim in sides:
        count = lax.axis_size(axis)
        ends = count - 1
        head = lax.slice_in_dim(cells, 0, width, axis=dim)
        tail = lax.slice_in_dim(cells, cells.shape[dim] - width, cells.shape[dim], axis=dim)
        cells = jnp.concatenate(
            [
                lax.ppermute(tail, axis, [(i, (i + 1) % count) for i in range(ends)]),
                cells,
                lax.ppermute(head, axis, [((i + 1) % count, i) for i in range(ends)]),
            ],
            axis=dim,
        )
    return cells


def spline_weights(fraction):
    rest = 1.0 - fraction
    square = fraction * fraction
    cube = square * fraction
    return [
        rest * rest * rest / 6.0,
        (3.0 * cube - 6.0 * square + 4.0) / 6.0,
        (-3.0 * cube + 3.0 * square + 3.0 * fraction + 1.0) / 6.0,
        cube / 6.0,
    ]


def knot_features(attitude, fraction, weights, reduced):
    basis = spline_weights(fraction)
    outer = [attitude[c] * attitude[e] for c, e in component_pairs]
    rows = []
    for j, d in spline_pairs:
        factor = weights * basis[j] * basis[j + d]
        for product in outer:
            rows.append(factor * product)
    for j in range(4):
        factor = weights * basis[j] * reduced
        for c in range(4):
            rows.append(factor * attitude[c])
    filler = jnp.zeros_like(fraction)
    while len(rows) < 128:
        rows.append(filler)
    return jnp.stack(rows, 0)


def collect(features, index, count):
    n_rows = index.shape[0]
    block = min(512, n_rows)
    steps = n_rows // block
    width = features.shape[0]
    feat_blocks = jnp.transpose(features.reshape(width, steps, block), (1, 0, 2))
    index_blocks = index.reshape(steps, block)
    columns = jnp.arange(count, dtype=jnp.int32)

    def add_block(total, pieces):
        feat, idx = pieces
        onehot = (idx[:, None] == columns[None, :]).astype(jnp.float32)
        return (
            total
            + jnp.dot(
                feat, onehot, precision=lax.Precision.HIGHEST, preferred_element_type=jnp.float32
            ),
            None,
        )

    total, _ = lax.scan(
        add_block, jnp.zeros((width, count), jnp.float32), (feat_blocks, index_blocks)
    )
    return total


def band_from(collected, count_out):
    padded = jnp.pad(collected, ((0, 0), (3, 3)))
    rows = []
    for d in range(4):
        for c in range(4):
            for e in range(4):
                q = component_pairs.index((min(c, e), max(c, e)))
                total = None
                for j in range(4 - d):
                    p = spline_pairs.index((j, d))
                    term = padded[p * 10 + q, 3 - j : 3 - j + count_out]
                    total = term if total is None else total + term
                rows.append(total)
    for c in range(4):
        total = None
        for j in range(4):
            term = padded[100 + 4 * j + c, 3 - j : 3 - j + count_out]
            total = term if total is None else total + term
        rows.append(total)
    return jnp.stack(rows, 0)


def source_rows(design, weights, resid):
    pieces = [weights * design[i] * design[j] for i, j in index_pairs]
    pieces = pieces + [weights * design[i] * resid for i in range(5)]
    return jnp.stack(pieces, 0)


def pick_sources(source_update, source_id):
    n_rows = source_id.shape[0]
    block = min(512, n_rows)
    steps = n_rows // block
    columns = jnp.arange(source_update.shape[1], dtype=jnp.int32)

    def pick_block(idx):
        onehot = (idx[:, None] == columns[None, :]).astype(jnp.float32)
        return lax.dot_general(
            source_update,
            onehot,
            (((1,), (1,)), ((), ())),
            precision=lax.Precision.HIGHEST,
            preferred_element_type=jnp.float32,
        )

    picked = lax.map(pick_block, source_id.reshape(steps, block))
    return jnp.transpose(picked, (1, 0, 2)).reshape(5, n_rows)


def solve_five(normals):
    entry = {}
    for n, (i, j) in enumerate(index_pairs):
        entry[j, i] = normals[n]
    for i in range(5):
        entry[i, i] = entry[i, i] + prior_source
    lower = {}
    for i in range(5):
        for j in range(i + 1):
            value = entry[i, j]
            for k in range(j):
                value = value - lower[i, k] * lower[j, k]
            if i == j:
                lower[i, i] = jnp.sqrt(value)
            else:
                lower[i, j] = value / lower[j, j]
    forward = []
    for i in range(5):
        value = normals[15 + i]
        for k in range(i):
            value = value - lower[i, k] * forward[k]
        forward.append(value / lower[i, i])
    solution = [None] * 5
    for i in range(4, -1, -1):
        value = forward[i]
        for k in range(i + 1, 5):
            value = value - lower[k, i] * solution[k]
        solution[i] = value / lower[i, i]
    return jnp.stack(solution, 0)


def apply_band(matrix, matrix_ext, padded, columns):
    result = prior_attitude * padded[:, 3 : 3 + columns]
    for d in range(4):
        block_mat = matrix[16 * d : 16 * d + 16].reshape(4, 4, columns)
        result = result + jnp.einsum(
            "abk,bk->ak",
            block_mat,
            padded[:, 3 + d : 3 + d + columns],
            precision=lax.Precision.HIGHEST,
        )
    for d in range(1, 4):
        block_mat = matrix_ext[16 * d : 16 * d + 16, 3 - d : 3 - d + columns].reshape(4, 4, columns)
        result = result + jnp.einsum(
            "bak,bk->ak",
            block_mat,
            padded[:, 3 - d : 3 - d + columns],
            precision=lax.Precision.HIGHEST,
        )
    return result


def body(
    attitude_design,
    source_design,
    scan_phase,
    obs_weight,
    obs_residual,
    source_id,
    knot_start,
    time_segment,
):
    contrib = source_rows(source_design, obs_weight, obs_residual)
    own_normals = collect(contrib, source_id, S_DEV)
    normals = lax.psum(own_normals, "tm")
    source_update = solve_five(normals)
    picked = pick_sources(source_update, source_id)
    reduced = obs_residual - jnp.sum(source_design * picked, axis=0)
    segment_of = time_segment[:, 0]
    seg_count = lax.axis_size("tm")
    knot_count = KS * seg_count
    width = KS
    features = knot_features(attitude_design, scan_phase, obs_weight, reduced)
    first = segment_of * KS + knot_start
    full_band = band_from(collect(features, first, knot_count), knot_count)
    partial_band = lax.psum_scatter(full_band, "tm", scatter_dimension=1, tiled=True)
    band = lax.psum(partial_band, "src")
    matrix = band[:64]
    rhs = band[64:68]
    rim = from_behind(matrix[:, width - 3 :], "tm", 1)
    matrix_ext = jnp.concatenate([rim, matrix], 1)

    def squares(resid):
        return lax.psum(jnp.sum(resid * resid), "tm")

    solution = jnp.zeros_like(rhs)
    resid = rhs
    direction = rhs
    norm_now = squares(resid)
    for step in range(ITERS):
        padded = with_halo(direction, (("tm", 1),), 3)
        image = apply_band(matrix, matrix_ext, padded, width)
        alpha = norm_now / lax.psum(jnp.sum(direction * image), "tm")
        solution = solution + alpha * direction
        resid = resid - alpha * image
        norm_next = squares(resid)
        direction = resid + norm_next / norm_now * direction
        norm_now = norm_next
    return (source_update, solution)


def solution(mesh):
    in_specs = (
        P(None, ("src", "tm")),
        P(None, ("src", "tm")),
        P(("src", "tm")),
        P(("src", "tm")),
        P(("src", "tm")),
        P(("src", "tm")),
        P(("src", "tm")),
        P(("src", "tm"), None),
    )
    out_specs = (P(None, "src"), P(None, "tm"))
    return jax.shard_map(body, mesh=mesh, in_specs=in_specs, out_specs=out_specs, check_vma=False)
```

profile of v0, /device:TPU:0, one launch (start us, length us, event | category | flops | bytes accessed | tf_op | source)
XLA Modules:
  0.0 381.2 jit_solution(8686215331941736714)
XLA Ops:
  7.2 1.5 fusion.143
  9.4 0.8 multiply_multiply_fusion.6
  10.7 12.4 %while.34 = (s32[]{:T(128)}, f32[20,2048]{1,0:T(8,128)S(1)}, f32[8,20,512]{2,1,0:T(8,128)S(1)}, s32[8,512]{1,0:T(8,128)S(1)}, s32[]{:T(128)}, /*index=5*/s32[]{:T(128)}) while((s32[]{:T(128)}, f32[20,2048]{1,0:T(8,128)S(1)}, f32[8,20,512]{2,1,0:T(8,128)S(1)}, s32[8,512]{1,0:T(8,128)S(1)}, s32[]{:T(128)}, ...), condition=%wide.region_1.2_spmd.clone, body=%wide.region_0.1_spmd.clone.sunk | while | flops 252788736 | bytes 415831 | solution.py:91
  10.8 1.5 fusion.160
  12.3 1.5 fusion.160
  13.8 1.5 fusion.160
  15.4 1.5 fusion.160
  16.9 1.5 fusion.160
  18.5 1.5 fusion.160
  20.0 1.5 fusion.160
  21.6 1.5 fusion.160
  24.8 36.7 %all-reduce.5.cloned.1.call-done = f32[20,2048]{1,0:T(8,128)} async-done(((f32[20,2048]{1,0:T(8,128)}), f32[20,2048]{1,0:T(8,128)}) %all-reduce.5.cloned.1.call-update) | async-done | bytes 163856 | tf_op jit(solution)/shard_map/psum | solution.py:209
  61.5 1.6 fusion.101
  63.1 1.3 fusion.102
  64.4 1.3 subtract_divide_fusion
  65.8 16.3 %while.33 = (s32[]{:T(128)}, f32[8,5,512]{2,1,0:T(8,128)S(1)}, s32[8,512]{1,0:T(8,128)S(1)}, f32[5,2048]{1,0:T(8,128)S(1)}, s32[]{:T(128)}) while((s32[]{:T(128)}, f32[8,5,512]{2,1,0:T(8,128)S(1)}, s32[8,512]{1,0:T(8,128)S(1)}, f32[5,2048]{1,0:T(8,128)S(1)}, s32[]{:T(128)}) %tuple.351), condition=%wide.region_4.5_spmd.clone, body=%wide.region_3.4_spmd.clone.sunk | while | flops 63963136 | bytes 88133 | solution.py:141
  65.8 2.0 fusion.158
  67.8 2.0 fusion.158
  69.8 2.0 fusion.158
  71.9 2.0 fusion.158
  73.9 2.0 fusion.158
  75.9 2.0 fusion.158
  78.0 2.0 fusion.158
  80.0 2.0 fusion.158
  83.6 1.0 fusion.148
  84.6 24.5 %stack.624 = f32[128,8,512]{2,0,1:T(8,128)} concatenate(f32[1,8,512]{2,0,1:T(1,128)S(1)} %bitcast.483, f32[1,8,512]{2,0,1:T(1,128)} %bitcast.534, f32[1,8,512]{2,0,1:T(1,128)} %bitcast.535, f32[1,8,512]{2,0,1:T(1,128)} %bitcast.536, f32[1,8,512]{2,0,1:T(1,128)S(1)} %bitcast.485, f32[1,8,512]{2,0,1:T(1,128)} %bitcast.537, f32[1,8,512]{2,0,1:T(1,128)} %bitcast.538, ...), dimensions={0} | concatenate | bytes 4194304 | tf_op jit(solution)/shard_map/stack | solution.py:68
  109.1 45.1 %while.35 = (s32[]{:T(128)}, f32[128,4096]{1,0:T(8,128)S(1)}, f32[8,128,512]{2,1,0:T(8,128)}, s32[8,512]{1,0:T(8,128)}, s32[]{:T(128)}, /*index=5*/s32[]{:T(128)}) while((s32[]{:T(128)}, f32[128,4096]{1,0:T(8,128)S(1)}, f32[8,128,512]{2,1,0:T(8,128)}, s32[8,512]{1,0:T(8,128)}, s32[]{:T(128)}, /*index=5*/s32[]{:T(128)}) %tuple.349), condition=%wide.region_7.8_spmd.clone, body=%wide.region_6.7_spmd.clone.sunk | while | flops 3224371200 | bytes 4463187 | solution.py:91
  109.8 4.9 %fusion.162 = f32[128,4096]{1,0:T(8,128)S(1)} fusion(s32[512]{0:T(512)S(1)} %bitcast.579, f32[128,4096]{1,0:T(8,128)S(1)} %get-tuple-element.605, pred[]{:T(512)S(6)} %compare.8, f32[8,128,512]{2,1,0:T(8,128)} %get-tuple-element.612, s32[]{:T(128)} %get-tuple-element.604), kind=kOutput, calls=%fused_computation.19.clone.1 | convolution fusion | flops 3224371200 | bytes 4459009 | tf_op jit(solution)/shard_map/while/body/eval_jaxpr/dot_general | solution.py:85
  114.7 0.7 constant_dynamic-slice_fusion.8
  115.4 4.9 %fusion.162 = f32[128,4096]{1,0:T(8,128)S(1)} fusion(s32[512]{0:T(512)S(1)} %bitcast.579, f32[128,4096]{1,0:T(8,128)S(1)} %get-tuple-element.605, pred[]{:T(512)S(6)} %compare.8, f32[8,128,512]{2,1,0:T(8,128)} %get-tuple-element.612, s32[]{:T(128)} %get-tuple-element.604), kind=kOutput, calls=%fused_computation.19.clone.1 | convolution fusion | flops 3224371200 | bytes 4459009 | tf_op jit(solution)/shard_map/while/body/eval_jaxpr/dot_general | solution.py:85
  120.3 0.7 constant_dynamic-slice_fusion.8
  121.1 4.9 %fusion.162 = f32[128,4096]{1,0:T(8,128)S(1)} fusion(s32[512]{0:T(512)S(1)} %bitcast.579, f32[128,4096]{1,0:T(8,128)S(1)} %get-tuple-element.605, pred[]{:T(512)S(6)} %compare.8, f32[8,128,512]{2,1,0:T(8,128)} %get-tuple-element.612, s32[]{:T(128)} %get-tuple-element.604), kind=kOutput, calls=%fused_computation.19.clone.1 | convolution fusion | flops 3224371200 | bytes 4459009 | tf_op jit(solution)/shard_map/while/body/eval_jaxpr/dot_general | solution.py:85
  125.9 0.7 constant_dynamic-slice_fusion.8
  126.7 4.9 %fusion.162 = f32[128,4096]{1,0:T(8,128)S(1)} fusion(s32[512]{0:T(512)S(1)} %bitcast.579, f32[128,4096]{1,0:T(8,128)S(1)} %get-tuple-element.605, pred[]{:T(512)S(6)} %compare.8, f32[8,128,512]{2,1,0:T(8,128)} %get-tuple-element.612, s32[]{:T(128)} %get-tuple-element.604), kind=kOutput, calls=%fused_computation.19.clone.1 | convolution fusion | flops 3224371200 | bytes 4459009 | tf_op jit(solution)/shard_map/while/body/eval_jaxpr/dot_general | solution.py:85
  132.3 4.9 %fusion.162 = f32[128,4096]{1,0:T(8,128)S(1)} fusion(s32[512]{0:T(512)S(1)} %bitcast.579, f32[128,4096]{1,0:T(8,128)S(1)} %get-tuple-element.605, pred[]{:T(512)S(6)} %compare.8, f32[8,128,512]{2,1,0:T(8,128)} %get-tuple-element.612, s32[]{:T(128)} %get-tuple-element.604), kind=kOutput, calls=%fused_computation.19.clone.1 | convolution fusion | flops 3224371200 | bytes 4459009 | tf_op jit(solution)/shard_map/while/body/eval_jaxpr/dot_general | solution.py:85
  137.9 4.9 %fusion.162 = f32[128,4096]{1,0:T(8,128)S(1)} fusion(s32[512]{0:T(512)S(1)} %bitcast.579, f32[128,4096]{1,0:T(8,128)S(1)} %get-tuple-element.605, pred[]{:T(512)S(6)} %compare.8, f32[8,128,512]{2,1,0:T(8,128)} %get-tuple-element.612, s32[]{:T(128)} %get-tuple-element.604), kind=kOutput, calls=%fused_computation.19.clone.1 | convolution fusion | flops 3224371200 | bytes 4459009 | tf_op jit(solution)/shard_map/while/body/eval_jaxpr/dot_general | solution.py:85
  143.5 4.9 %fusion.162 = f32[128,4096]{1,0:T(8,128)S(1)} fusion(s32[512]{0:T(512)S(1)} %bitcast.579, f32[128,4096]{1,0:T(8,128)S(1)} %get-tuple-element.605, pred[]{:T(512)S(6)} %compare.8, f32[8,128,512]{2,1,0:T(8,128)} %get-tuple-element.612, s32[]{:T(128)} %get-tuple-element.604), kind=kOutput, calls=%fused_computation.19.clone.1 | convolution fusion | flops 3224371200 | bytes 4459009 | tf_op jit(solution)/shard_map/while/body/eval_jaxpr/dot_general | solution.py:85
  149.1 4.9 %fusion.162 = f32[128,4096]{1,0:T(8,128)S(1)} fusion(s32[512]{0:T(512)S(1)} %bitcast.579, f32[128,4096]{1,0:T(8,128)S(1)} %get-tuple-element.605, pred[]{:T(512)S(6)} %compare.8, f32[8,128,512]{2,1,0:T(8,128)} %get-tuple-element.612, s32[]{:T(128)} %get-tuple-element.604), kind=kOutput, calls=%fused_computation.19.clone.1 | convolution fusion | flops 3224371200 | bytes 4459009 | tf_op jit(solution)/shard_map/while/body/eval_jaxpr/dot_general | solution.py:85
  157.2 7.2 %stack.625 = f32[68,4096]{1,0:T(8,128)} concatenate(f32[1,4096]{1,0:T(1,128)S(1)} %get-tuple-element.269, f32[1,4096]{1,0:T(1,128)S(1)} %get-tuple-element.268, f32[1,4096]{1,0:T(1,128)S(1)} %get-tuple-element.267, f32[1,4096]{1,0:T(1,128)S(1)} %get-tuple-element.266, f32[1,4096]{1,0:T(1,128)S(1)} %get-tuple-element.268, f32[1,4096]{1,0:T(1,128)S(1)} %get-tuple-element.265, ...), dimensions={0} | concatenate | bytes 2228224 | tf_op jit(solution)/shard_map/stack | solution.py:116
  164.5 29.0 %reduce-scatter.2.cloned.1.call-done = f32[68,1024]{1,0:T(8,128)} async-done(((f32[68,4096]{1,0:T(8,128)}), f32[68,1024]{1,0:T(8,128)}) %reduce-scatter.2.cloned.1.call-update) | async-done | bytes 278544 | tf_op jit(solution)/shard_map/reduce_scatter | solution.py:220
  193.5 55.2 %all-reduce.7.cloned.1.call-done = f32[68,1024]{1,0:T(8,128)} async-done(((f32[68,1024]{1,0:T(8,128)}), f32[68,1024]{1,0:T(8,128)}) %all-reduce.7.cloned.1.call-update) | async-done | bytes 278544 | tf_op jit(solution)/shard_map/psum | solution.py:221
  248.8 0.8 fusion.142
  249.6 1.3 collective-permute-start
  250.9 4.5 %collective-permute-start.1 = (f32[4,3]{1,0:T(4,128)S(1)}, f32[4,3]{1,0:T(4,128)S(1)}, u32[]{:S(2)}, u32[]{:S(2)}) collective-permute-start(f32[4,3]{1,0:T(4,128)S(1)} %get-tuple-element.277), channel_id=1, source_target_pairs={{0,1},{1,2},{2,3},{4,5},{5,6},{6,7},{8,9},{9,10},{10,11},{12,13},{... | collective-permute-start | bytes 152 | tf_op jit(solution)/shard_map/ppermute | solution.py:32
  255.4 1.0 fusion.141
  256.5 0.8 slice.1000
  257.3 3.4 collective-permute-start.2
  260.7 0.8 slice_bitcast_fusion
  263.3 11.7 %all-reduce.1 = (f32[]{:T(128)}, f32[]{:T(128)}) all-reduce(f32[]{:T(128)} %get-tuple-element.131, f32[]{:T(128)} %get-tuple-element.130), channel_id=1, replica_groups=mesh['src'=8,'tm'=4] {'tm'}, use_global_device_ids=true, to_apply=%region_11.12 | all-reduce | flops 2 | bytes 16 | tf_op jit(solution)/shard_map/psum | solution.py:228
  276.8 9.3 %psum.74 = f32[]{:T(128)} all-reduce(f32[]{:T(128)} %multiply_reduce_fusion.33), channel_id=1, replica_groups=mesh['src'=8,'tm'=4] {'tm'}, use_global_device_ids=true, to_apply=%region_15.16 | all-reduce | flops 1 | bytes 8 | tf_op jit(solution)/shard_map/psum | solution.py:228
  287.5 1.3 collective-permute-start.3
  288.8 4.5 %collective-permute-start.4 = (f32[4,3]{1,0:T(4,128)S(1)}, f32[4,3]{1,0:T(4,128)S(1)}, u32[]{:S(2)}, u32[]{:S(2)}) collective-permute-start(f32[4,3]{1,0:T(4,128)S(1)} %get-tuple-element.417), channel_id=1, source_target_pairs={{0,1},{1,2},{2,3},{4,5},{5,6},{6,7},{8,9},{9,10},{10,11},{12,13},{... | collective-permute-start | bytes 152 | tf_op jit(solution)/shard_map/ppermute | solution.py:32
  293.3 1.3 collective-permute-done.4
  295.7 11.8 %psum.75 = f32[]{:T(128)} all-reduce(f32[]{:T(128)} %get-tuple-element.162), channel_id=1, replica_groups=mesh['src'=8,'tm'=4] {'tm'}, use_global_device_ids=true, to_apply=%region_17.18 | all-reduce | flops 1 | bytes 8 | tf_op jit(solution)/shard_map/psum | solution.py:237
  309.4 9.2 %psum.76 = f32[]{:T(128)} all-reduce(f32[]{:T(128)} %get-tuple-element.160), channel_id=1, replica_groups=mesh['src'=8,'tm'=4] {'tm'}, use_global_device_ids=true, to_apply=%region_19.20 | all-reduce | flops 1 | bytes 8 | tf_op jit(solution)/shard_map/psum | solution.py:228
  320.0 1.3 collective-permute-start.5
  321.3 4.5 %collective-permute-start.6 = (f32[4,3]{1,0:T(4,128)S(1)}, f32[4,3]{1,0:T(4,128)S(1)}, u32[]{:S(2)}, u32[]{:S(2)}) collective-permute-start(f32[4,3]{1,0:T(4,128)S(1)} %get-tuple-element.412), channel_id=1, source_target_pairs={{0,1},{1,2},{2,3},{4,5},{5,6},{6,7},{8,9},{9,10},{10,11},{12,13},{... | collective-permute-start | bytes 152 | tf_op jit(solution)/shard_map/ppermute | solution.py:32
  325.9 1.3 collective-permute-done.6
  328.2 11.9 %psum.77 = f32[]{:T(128)} all-reduce(f32[]{:T(128)} %get-tuple-element.158), channel_id=1, replica_groups=mesh['src'=8,'tm'=4] {'tm'}, use_global_device_ids=true, to_apply=%region_21.22 | all-reduce | flops 1 | bytes 8 | tf_op jit(solution)/shard_map/psum | solution.py:237
  341.9 9.2 %psum.78 = f32[]{:T(128)} all-reduce(f32[]{:T(128)} %multiply_reduce_fusion.29), channel_id=1, replica_groups=mesh['src'=8,'tm'=4] {'tm'}, use_global_device_ids=true, to_apply=%region_23.24 | all-reduce | flops 1 | bytes 8 | tf_op jit(solution)/shard_map/psum | solution.py:228
  352.5 1.3 collective-permute-start.7
  353.8 4.5 %collective-permute-start.8 = (f32[4,3]{1,0:T(4,128)S(1)}, f32[4,3]{1,0:T(4,128)S(1)}, u32[]{:S(2)}, u32[]{:S(2)}) collective-permute-start(f32[4,3]{1,0:T(4,128)S(1)} %get-tuple-element.407), channel_id=1, source_target_pairs={{0,1},{1,2},{2,3},{4,5},{5,6},{6,7},{8,9},{9,10},{10,11},{12,13},{... | collective-permute-start | bytes 152 | tf_op jit(solution)/shard_map/ppermute | solution.py:32
  358.4 1.3 collective-permute-done.8
  360.7 12.0 %psum.79 = f32[]{:T(128)} all-reduce(f32[]{:T(128)} %fusion.71), channel_id=1, replica_groups=mesh['src'=8,'tm'=4] {'tm'}, use_global_device_ids=true, to_apply=%region_25.26 | all-reduce | flops 1 | bytes 8 | tf_op jit(solution)/shard_map/psum | solution.py:237
  (132 shorter events, 19.2 us)
Async XLA Ops:
  7.2 54.3 %all-reduce.5.cloned.1.call-start = ((), (), s32[]{:S(2)}) async-start(), calls=%async_computation.1 | async-start | bytes 393216 | tf_op jit(solution)/shard_map/psum | solution.py:209
  10.7 13.3 %copy-start.4 = (f32[4,4096]{1,0:T(4,128)S(1)}, f32[4,4096]{1,0:T(4,128)}, u32[]{:S(2)}) copy-start(f32[4,4096]{1,0:T(4,128)} %param.14) | copy-start | bytes 196612
  10.7 13.4 %copy-start.9 = (s32[4096,1]{0,1:T(1,128)S(1)}, s32[4096,1]{0,1:T(1,128)}, u32[]{:S(2)}) copy-start(s32[4096,1]{0,1:T(1,128)} %param.21) | copy-start | bytes 49156
  10.7 13.4 %copy-start.8 = (s32[4096]{0:T(1024)S(1)}, s32[4096]{0:T(1024)}, u32[]{:S(2)}) copy-start(s32[4096]{0:T(1024)} %param.20) | copy-start | bytes 49156
  23.1 0.7 copy-start.2
  23.8 169.7 %reduce-scatter.2.cloned.1.call-start = ((), (), s32[]{:S(2)}) async-start(), calls=%async_computation.2 | async-start | bytes 1474560 | tf_op jit(solution)/shard_map/reduce_scatter | solution.py:220
  65.7 16.3 %copy-start.1 = (f32[5,4096]{1,0:T(8,128)S(1)}, f32[5,4096]{1,0:T(8,128)}, u32[]{:S(2)}) copy-start(f32[5,4096]{1,0:T(8,128)} %param.15) | copy-start | bytes 245764
  65.7 16.4 %copy-start.3 = (f32[4096]{0:T(1024)S(1)}, f32[4096]{0:T(1024)}, u32[]{:S(2)}) copy-start(f32[4096]{0:T(1024)} %param.17) | copy-start | bytes 49156
  65.7 16.4 %copy-start.6 = (f32[4096]{0:T(1024)S(1)}, f32[4096]{0:T(1024)}, u32[]{:S(2)}) copy-start(f32[4096]{0:T(1024)} %param.18) | copy-start | bytes 49156
  65.7 16.4 %copy-start.7 = (f32[4096]{0:T(1024)S(1)}, f32[4096]{0:T(1024)}, u32[]{:S(2)}) copy-start(f32[4096]{0:T(1024)} %param.16) | copy-start | bytes 49156
  82.0 1.4 copy-start.5
  164.5 84.3 %all-reduce.7.cloned.1.call-start = ((), (), s32[]{:S(2)}) async-start(), calls=%async_computation.3 | async-start | bytes 589824 | tf_op jit(solution)/shard_map/psum | solution.py:221
  248.7 13.5 %slice-start = ((f32[68,1024]{1,0:T(8,128)}), f32[64,1024]{1,0:T(8,128)S(1)}, s32[]{:S(2)}) async-start(f32[68,1024]{1,0:T(8,128)} %all-reduce.7.cloned.1.call-done), calls=%async_computation.4 | async-start | bytes 524288 | tf_op jit(solution)/shard_map/slice | solution.py:222
  248.7 13.8 %copy-start = (f32[68,1024]{1,0:T(8,128)S(1)}, f32[68,1024]{1,0:T(8,128)}, u32[]{:S(2)}) copy-start(f32[68,1024]{1,0:T(8,128)} %all-reduce.7.cloned.1.call-done) | copy-start | bytes 835588
  249.6 11.9 %collective-permute-start = (f32[4,3]{1,0:T(4,128)S(1)}, f32[4,3]{1,0:T(4,128)S(1)}, u32[]{:S(2)}, u32[]{:S(2)}) collective-permute-start(f32[4,3]{1,0:T(4,128)S(1)} %get-tuple-element.276), channel_id=1, source_target_pairs={{1,0},{2,1},{3,2},{5,4},{6,5},{7,6},{9,8},{10,9},{11,10},{13,12},{... | collective-permute-start | bytes 152 | tf_op jit(solution)/shard_map/ppermute | solution.py:34
  250.9 10.6 %collective-permute-start.1 = (f32[4,3]{1,0:T(4,128)S(1)}, f32[4,3]{1,0:T(4,128)S(1)}, u32[]{:S(2)}, u32[]{:S(2)}) collective-permute-start(f32[4,3]{1,0:T(4,128)S(1)} %get-tuple-element.277), channel_id=1, source_target_pairs={{0,1},{1,2},{2,3},{4,5},{5,6},{6,7},{8,9},{9,10},{10,11},{12,13},{... | collective-permute-start | bytes 152 | tf_op jit(solution)/shard_map/ppermute | solution.py:32
  257.3 5.0 %collective-permute-start.2 = (f32[64,3]{1,0:T(8,128)S(1)}, f32[64,3]{1,0:T(8,128)S(1)}, u32[]{:S(2)}, u32[]{:S(2)}) collective-permute-start(f32[64,3]{1,0:T(8,128)S(1)} %slice.1000), channel_id=1, source_target_pairs={{0,1},{1,2},{2,3},{4,5},{5,6},{6,7},{8,9},{9,10},{10,11},{12,13},{... | collective-permute-start | bytes 2312 | tf_op jit(solution)/shard_map/ppermute | solution.py:21
  287.5 5.9 %collective-permute-start.3 = (f32[4,3]{1,0:T(4,128)S(1)}, f32[4,3]{1,0:T(4,128)S(1)}, u32[]{:S(2)}, u32[]{:S(2)}) collective-permute-start(f32[4,3]{1,0:T(4,128)S(1)} %get-tuple-element.416), channel_id=1, source_target_pairs={{1,0},{2,1},{3,2},{5,4},{6,5},{7,6},{9,8},{10,9},{11,10},{13,12},{... | collective-permute-start | bytes 152 | tf_op jit(solution)/shard_map/ppermute | solution.py:34
  288.8 5.8 %collective-permute-start.4 = (f32[4,3]{1,0:T(4,128)S(1)}, f32[4,3]{1,0:T(4,128)S(1)}, u32[]{:S(2)}, u32[]{:S(2)}) collective-permute-start(f32[4,3]{1,0:T(4,128)S(1)} %get-tuple-element.417), channel_id=1, source_target_pairs={{0,1},{1,2},{2,3},{4,5},{5,6},{6,7},{8,9},{9,10},{10,11},{12,13},{... | collective-permute-start | bytes 152 | tf_op jit(solution)/shard_map/ppermute | solution.py:32
  320.0 5.9 %collective-permute-start.5 = (f32[4,3]{1,0:T(4,128)S(1)}, f32[4,3]{1,0:T(4,128)S(1)}, u32[]{:S(2)}, u32[]{:S(2)}) collective-permute-start(f32[4,3]{1,0:T(4,128)S(1)} %get-tuple-element.411), channel_id=1, source_target_pairs={{1,0},{2,1},{3,2},{5,4},{6,5},{7,6},{9,8},{10,9},{11,10},{13,12},{... | collective-permute-start | bytes 152 | tf_op jit(solution)/shard_map/ppermute | solution.py:34
  321.3 5.8 %collective-permute-start.6 = (f32[4,3]{1,0:T(4,128)S(1)}, f32[4,3]{1,0:T(4,128)S(1)}, u32[]{:S(2)}, u32[]{:S(2)}) collective-permute-start(f32[4,3]{1,0:T(4,128)S(1)} %get-tuple-element.412), channel_id=1, source_target_pairs={{0,1},{1,2},{2,3},{4,5},{5,6},{6,7},{8,9},{9,10},{10,11},{12,13},{... | collective-permute-start | bytes 152 | tf_op jit(solution)/shard_map/ppermute | solution.py:32
  352.5 5.9 %collective-permute-start.7 = (f32[4,3]{1,0:T(4,128)S(1)}, f32[4,3]{1,0:T(4,128)S(1)}, u32[]{:S(2)}, u32[]{:S(2)}) collective-permute-start(f32[4,3]{1,0:T(4,128)S(1)} %get-tuple-element.406), channel_id=1, source_target_pairs={{1,0},{2,1},{3,2},{5,4},{6,5},{7,6},{9,8},{10,9},{11,10},{13,12},{... | collective-permute-start | bytes 152 | tf_op jit(solution)/shard_map/ppermute | solution.py:34
  353.8 5.8 %collective-permute-start.8 = (f32[4,3]{1,0:T(4,128)S(1)}, f32[4,3]{1,0:T(4,128)S(1)}, u32[]{:S(2)}, u32[]{:S(2)}) collective-permute-start(f32[4,3]{1,0:T(4,128)S(1)} %get-tuple-element.407), channel_id=1, source_target_pairs={{0,1},{1,2},{2,3},{4,5},{5,6},{6,7},{8,9},{9,10},{10,11},{12,13},{... | collective-permute-start | bytes 152 | tf_op jit(solution)/shard_map/ppermute | solution.py:32
Sparse Core Ops, SparseCore 0:
  23.9 37.4 all-reduce.4
  164.6 28.8 reduce-scatter.1
  196.9 51.7 all-reduce.6
where the time goes:
time: 385 us; the launch traced here: 381 us
  waiting for transfers between devices  125 us (32%)
  blocking collectives  74.9 us (19%)
  matrix products  67.1 us (17%)
  local copies, waits for them, and re-layouts  45.6 us (12%)
  starting transfers between devices  27 us (7%)
  between operations  23.2 us (6%)
  other arithmetic  17.3 us (4%)
    psum x1, waiting for transfers between devices, body(): band = lax.psum(partial_band, 'src')  55.2 us
    dot_general x16, matrix products, add_block(): jnp.dot(feat, onehot, precision=lax.Precision.HIGHEST, preferred_element_...  51 us
    psum x4, blocking collectives, squares(): return lax.psum(jnp.sum(resid * resid), 'tm')  39.3 us
    psum x1, waiting for transfers between devices, body(): normals = lax.psum(own_normals, 'tm')  36.7 us
    psum x3, blocking collectives, body(): alpha = norm_now / lax.psum(jnp.sum(direction * image), 'tm')  35.7 us
    reduce_scatter x1, waiting for transfers between devices, body(): lax.psum_scatter(full_band, 'tm', scatter_dimension=1, tiled=True)  29 us
    another operation x3, local copies, waits for them, and re-layouts, knot_features(): return jnp.stack(rows, 0)  24.5 us
    ppermute x4, starting transfers between devices, with_halo(): lax.ppermute(tail, axis, [(i, (i + 1) % count) for i in range(ends)])  18.2 us
  transfers between devices with their start and end apart: 12, of which 7 were waited for; matrix products, arithmetic and copies ran while one was open for 1% of the time, Pallas kernels for 0%

commit v1 on v0

v1 whole, which is shorter than its diff:
```python
import functools

import jax
import jax.numpy as jnp
from jax import lax
from jax.experimental import pallas as pl
from jax.experimental.pallas import tpu as pltpu
from jax.sharding import PartitionSpec as P

KS = 1024
S_DEV = 2048
ITERS = 4
ROWS = 48
SRC_GROUPS = 8
SRC_WIDE = S_DEV // SRC_GROUPS
MESH = pl.DeviceIdType.MESH

prior_source = 1.0
prior_attitude = 1.0
index_pairs = [(i, j) for i in range(5) for j in range(i, 5)]
component_pairs = [(c, e) for c in range(4) for e in range(c, 4)]
NT = (((1,), (1,)), ((), ()))


def split(x):
    high = x.astype(jnp.bfloat16)
    low = (x - high.astype(jnp.float32)).astype(jnp.bfloat16)
    return high, low


def onehot(count, index, base):
    place = lax.broadcasted_iota(jnp.int32, (count, index.shape[1]), 0) + base
    return jnp.where(place == index, 1.0, 0.0).astype(jnp.bfloat16)


def source_kernel(design_ref, weight_ref, resid_ref, id_ref, out_ref, lhs):
    q = [design_ref[i : i + 1, :] for i in range(5)]
    w = weight_ref[...]
    r = resid_ref[...]
    wq = [w * q[i] for i in range(5)]
    rows = [wq[i] * q[j] for i, j in index_pairs] + [wq[i] * r for i in range(5)]
    rows += [jnp.zeros_like(w)] * 4
    high, low = split(jnp.concatenate(rows, 0))
    both = jnp.concatenate([high.astype(jnp.float32), low.astype(jnp.float32)], 0)
    ids = id_ref[...]
    group = ids // SRC_WIDE
    for a in range(SRC_GROUPS):
        lhs[48 * a : 48 * a + 48, :] = jnp.where(group == a, both, 0.0).astype(jnp.bfloat16)
    hot = onehot(SRC_WIDE, ids % SRC_WIDE, 0)
    got = lax.dot_general(lhs[...], hot, NT, preferred_element_type=jnp.float32)
    for a in range(SRC_GROUPS):
        out_ref[a] = got[48 * a : 48 * a + 24] + got[48 * a + 24 : 48 * a + 48]


def solve_five(normals):
    entry = {}
    for n, (i, j) in enumerate(index_pairs):
        entry[j, i] = normals[n]
    for i in range(5):
        entry[i, i] = entry[i, i] + prior_source
    lower = {}
    for i in range(5):
        for j in range(i + 1):
            value = entry[i, j]
            for k in range(j):
                value = value - lower[i, k] * lower[j, k]
            if i == j:
                lower[i, i] = jnp.sqrt(value)
            else:
                lower[i, j] = value / lower[j, j]
    forward = []
    for i in range(5):
        value = normals[15 + i]
        for k in range(i):
            value = value - lower[i, k] * forward[k]
        forward.append(value / lower[i, i])
    result = [None] * 5
    for i in range(4, -1, -1):
        value = forward[i]
        for k in range(i + 1, 5):
            value = value - lower[k, i] * result[k]
        result[i] = value / lower[i, i]
    return result


def greet(peers):
    barrier = pltpu.get_barrier_semaphore()
    for peer in peers:
        pl.semaphore_signal(barrier, inc=1, device_id=peer, device_id_type=MESH)
    pl.semaphore_wait(barrier, len(peers))


def send(src, dst, sems, slot, peer):
    copy = pltpu.make_async_remote_copy(
        src_ref=src,
        dst_ref=dst,
        send_sem=sems.at[0, slot],
        recv_sem=sems.at[1, slot],
        device_id=peer,
        device_id_type=MESH,
    )
    copy.start()
    return copy


def normals_kernel(n_tm, own_ref, full_ref, update_ref, landed, gathered, sem_a, sem_b):
    me_s, me_t = lax.axis_index("src"), lax.axis_index("tm")
    part = SRC_GROUPS // n_tm
    at = [(me_s, lax.rem(me_t + o, n_tm)) for o in range(1, n_tm)]
    greet(at)
    copies = []
    for o in range(1, n_tm):
        copies.append(
            send(own_ref.at[pl.ds(at[o - 1][1] * part, part)], landed.at[o - 1], sem_a, o - 1, at[o - 1])
        )
    total = own_ref[pl.ds(me_t * part, part)]
    for o in range(1, n_tm):
        copies[o - 1].wait_recv()
        total = total + landed[o - 1]
    solved = solve_five([total[:, n, :] for n in range(20)])
    mine = pl.ds(me_t * part, part)
    for i in range(5):
        for g in range(part):
            gathered[me_t * part + g, i : i + 1, :] = solved[i][g : g + 1, :]
    for g in range(part):
        gathered[me_t * part + g, 5:8, :] = jnp.zeros((3, SRC_WIDE), jnp.float32)
    more = []
    for o in range(1, n_tm):
        more.append(send(gathered.at[mine], gathered.at[mine], sem_b, o - 1, at[o - 1]))
    for copy in copies:
        copy.wait_send()
    for copy in more:
        copy.wait()
    for a in range(SRC_GROUPS):
        block = gathered[a]
        full_ref[a] = block
        update_ref[:, a * SRC_WIDE : (a + 1) * SRC_WIDE] = block[0:5]


def knot_kernel(
    n_seg,
    full_ref,
    attitude_ref,
    design_ref,
    phase_ref,
    weight_ref,
    resid_ref,
    id_ref,
    start_ref,
    segment_ref,
    out_ref,
    feat,
    lhs,
    acc,
):
    n_obs = phase_ref.shape[1]
    ids = id_ref[...]
    group = ids // SRC_WIDE
    hot = onehot(SRC_WIDE, ids % SRC_WIDE, 0)
    table = full_ref[...].reshape(SRC_GROUPS * 8, SRC_WIDE)
    high, low = split(table)
    picks = jnp.dot(high, hot, preferred_element_type=jnp.float32) + jnp.dot(
        low, hot, preferred_element_type=jnp.float32
    )
    picked = jnp.zeros((8, n_obs), jnp.float32)
    for a in range(SRC_GROUPS):
        picked = picked + jnp.where(group == a, picks[8 * a : 8 * a + 8], 0.0)
    fitted = jnp.sum(design_ref[...] * picked[0:5], axis=0, keepdims=True)
    reduced = resid_ref[...] - fitted

    t = phase_ref[...]
    w = weight_ref[...]
    rest = 1.0 - t
    square = t * t
    cube = square * t
    basis = [
        rest * rest * rest / 6.0,
        (3.0 * cube - 6.0 * square + 4.0) / 6.0,
        (-3.0 * cube + 3.0 * square + 3.0 * t + 1.0) / 6.0,
        cube / 6.0,
    ]
    att = attitude_ref[...]
    outer = jnp.concatenate([att[c : c + 1] * att[e : e + 1] for c, e in component_pairs], 0)
    top = 0
    for j in range(4):
        scaled = w * basis[j]
        pieces = [att * (scaled * reduced)]
        for d in range(4 - j):
            pieces.append(outer * (scaled * basis[j + d]))
        size = 44 - 10 * j
        room = (48, 40, 24, 16)[j]
        if room > size:
            pieces.append(jnp.zeros((room - size, n_obs), jnp.float32))
        block_high, block_low = split(jnp.concatenate(pieces, 0))
        feat[top : top + room, :] = block_high.astype(jnp.float32)
        feat[128 + top : 128 + top + room, :] = block_low.astype(jnp.float32)
        top += room

    segment = segment_ref[...]
    for s in range(n_seg):
        lhs[256 * s : 256 * s + 256, :] = jnp.where(segment == s, feat[...], 0.0).astype(
            jnp.bfloat16
        )
    start = start_ref[...]

    def tile(n, carry):
        knots = onehot(256, start, n * 256)
        place = pl.ds(pl.multiple_of(n * 256, 256), 256)
        acc[:, place] = lax.dot_general(lhs[...], knots, NT, preferred_element_type=jnp.float32)
        return carry

    lax.fori_loop(0, KS // 256, tile, 0)

    lane = lax.broadcasted_iota(jnp.int32, (1, KS), 1)
    before = [None] * 4
    for s in range(n_seg):
        total = None
        top = 0
        for j in range(4):
            room = (48, 40, 24, 16)[j]
            base = 256 * s + top
            value = acc[base : base + room, :] + acc[base + 128 : base + 128 + room, :]
            top += room
            if j == 0:
                total = value
                continue
            size = 44 - 10 * j
            value = pltpu.roll(value, j, 1)
            carried = 0.0 if before[j] is None else before[j]
            before[j] = value
            value = jnp.where(lane < j, carried, value)
            if room > size:
                value = jnp.where(lax.broadcasted_iota(jnp.int32, (room, 1), 0) < size, value, 0.0)
            total = total + jnp.concatenate([value, jnp.zeros((48 - room, KS), jnp.float32)], 0) if room < 48 else total + value
        out_ref[s] = total.reshape(ROWS, 8, 128)


def shifted(x, by):
    lane = lax.broadcasted_iota(jnp.int32, x.shape, 2)
    turned = pltpu.roll(x, (128 - by) % 128, 2)
    if by > 0:
        return jnp.where(lane >= 128 - by, pltpu.roll(turned, 15, 1), turned)
    return jnp.where(lane < -by, pltpu.roll(turned, 1, 1), turned)


def attitude_kernel(
    n_src, n_tm, part_ref, out_ref, rs1, s1, rs2, full, stage, halo, ext, red, red_in,
    sem_a, sem_b, sem_c, sem_d, sem_e,
):
    me_s, me_t = lax.axis_index("src"), lax.axis_index("tm")
    rows = ROWS // n_src
    side = [(lax.rem(me_s + o, n_src), me_t) for o in range(1, n_src)]
    line = [(me_s, lax.rem(me_t + o, n_tm)) for o in range(1, n_tm)]
    greet(side + line)

    copies = []
    for o in range(1, n_src):
        peer = side[o - 1]
        copies.append(
            send(part_ref.at[:, pl.ds(peer[0] * rows, rows)], rs1.at[o - 1], sem_a, o - 1, peer)
        )
    total = part_ref[:, pl.ds(me_s * rows, rows)]
    for o in range(1, n_src):
        copies[o - 1].wait_recv()
        total = total + rs1[o - 1]
    s1[...] = total
    second = []
    for o in range(1, n_tm):
        peer = line[o - 1]
        second.append(send(s1.at[peer[1]], rs2.at[o - 1], sem_b, o - 1, peer))
    total = s1[me_t]
    for o in range(1, n_tm):
        second[o - 1].wait_recv()
        total = total + rs2[o - 1]
    mine = pl.ds(me_s * rows, rows)
    full[mine] = total
    third = []
    for o in range(1, n_src):
        third.append(send(full.at[mine], full.at[mine], sem_c, o - 1, side[o - 1]))
    for copy in copies + second:
        copy.wait_send()
    for copy in third:
        copy.wait()

    whole = full[...]
    stage[0] = whole[:, 0, :]
    stage[1] = whole[:, 7, :]
    ahead, behind = line[0], line[n_tm - 2]
    to_behind = send(stage.at[0], halo.at[0], sem_d, 0, behind)
    to_ahead = send(stage.at[1], halo.at[1], sem_d, 1, ahead)
    ext[:, 0:8, :] = whole
    ext[:, 8:16, :] = jnp.zeros((ROWS, 8, 128), jnp.float32)
    to_behind.wait()
    to_ahead.wait()
    ext[:, 8, :] = halo[0] * jnp.where(me_t < n_tm - 1, 1.0, 0.0)
    ext[:, 15, :] = halo[1] * jnp.where(me_t > 0, 1.0, 0.0)

    row = lax.broadcasted_iota(jnp.int32, (1, 16, 128), 1)
    kept = jnp.where(row < 8, 1.0, 0.0)
    kept = kept + jnp.where(row == 8, 1.0, 0.0) * jnp.where(me_t < n_tm - 1, 1.0, 0.0)
    kept = kept + jnp.where(row == 15, 1.0, 0.0) * jnp.where(me_t > 0, 1.0, 0.0)
    columns = []
    for d in range(4):
        for e in range(4):
            columns.append(
                jnp.stack(
                    [
                        ext[4 + 10 * d + component_pairs.index((min(c, e), max(c, e)))]
                        for c in range(4)
                    ],
                    0,
                )
            )

    def multiply(d, x):
        value = columns[4 * d] * x[0:1]
        for e in range(1, 4):
            value = value + columns[4 * d + e] * x[e : e + 1]
        return value

    def image_of(x):
        value = prior_attitude * x + multiply(0, x)
        for d in range(1, 4):
            value = value + multiply(d, shifted(x, d)) + shifted(multiply(d, x), -d)
        return value * kept

    resid = ext[0:4]
    direction = resid
    field = None
    image = None
    alpha = None
    gamma_old = None
    for step in range(ITERS):
        applied = image_of(resid)
        inner = resid[:, 0:8, :]
        red[step, 0] = jnp.sum(inner * inner, axis=0)
        red[step, 1] = jnp.sum(inner * applied[:, 0:8, :], axis=0)
        sums = []
        for o in range(1, n_tm):
            sums.append(
                send(red.at[step], red_in.at[step, o - 1], sem_e, step * (n_tm - 1) + o - 1, line[o - 1])
            )
        value = red[step]
        for o in range(1, n_tm):
            sums[o - 1].wait()
            value = value + red_in[step, o - 1]
        gamma = jnp.sum(value[0:1], axis=(1, 2), keepdims=True)
        delta = jnp.sum(value[1:2], axis=(1, 2), keepdims=True)
        if step == 0:
            alpha = gamma / delta
            direction, image = resid, applied
            field = alpha * direction
        else:
            beta = gamma / gamma_old
            alpha = gamma / (delta - beta * (gamma / alpha))
            direction = resid + beta * direction
            image = applied + beta * image
            field = field + alpha * direction
        resid = resid - alpha * image
        gamma_old = gamma
    out_ref[...] = field[:, 0:8, :]


def vmem(count):
    return [pl.BlockSpec(memory_space=pltpu.VMEM)] * count


def body(
    n_src,
    n_tm,
    attitude_design,
    source_design,
    scan_phase,
    obs_weight,
    obs_residual,
    source_id,
    knot_start,
    time_segment,
):
    n_obs = scan_phase.shape[0]
    f32 = jnp.float32
    flat = lambda x: x.reshape(1, n_obs)
    phase, weight, resid = flat(scan_phase), flat(obs_weight), flat(obs_residual)
    ids, start, segment = flat(source_id), flat(knot_start), flat(time_segment)
    limit = pltpu.CompilerParams(vmem_limit_bytes=56 * 1024 * 1024)
    own = pl.pallas_call(
        source_kernel,
        out_shape=jax.ShapeDtypeStruct((SRC_GROUPS, 24, SRC_WIDE), f32),
        in_specs=vmem(4),
        out_specs=vmem(1)[0],
        scratch_shapes=[pltpu.VMEM((48 * SRC_GROUPS, n_obs), jnp.bfloat16)],
        compiler_params=limit,
    )(source_design, weight, resid, ids)
    part = SRC_GROUPS // n_tm
    full, update = pl.pallas_call(
        functools.partial(normals_kernel, n_tm),
        out_shape=[
            jax.ShapeDtypeStruct((SRC_GROUPS, 8, SRC_WIDE), f32),
            jax.ShapeDtypeStruct((5, S_DEV), f32),
        ],
        in_specs=vmem(1),
        out_specs=vmem(2),
        scratch_shapes=[
            pltpu.VMEM((n_tm - 1, part, 24, SRC_WIDE), f32),
            pltpu.VMEM((SRC_GROUPS, 8, SRC_WIDE), f32),
            pltpu.SemaphoreType.DMA((2, n_tm - 1)),
            pltpu.SemaphoreType.DMA((2, n_tm - 1)),
        ],
        compiler_params=pltpu.CompilerParams(collective_id=0, has_side_effects=True),
    )(own)
    partial_band = pl.pallas_call(
        functools.partial(knot_kernel, n_tm),
        out_shape=jax.ShapeDtypeStruct((n_tm, ROWS, 8, 128), f32),
        in_specs=vmem(9),
        out_specs=vmem(1)[0],
        scratch_shapes=[
            pltpu.VMEM((256, n_obs), f32),
            pltpu.VMEM((256 * n_tm, n_obs), jnp.bfloat16),
            pltpu.VMEM((256 * n_tm, KS), f32),
        ],
        compiler_params=limit,
    )(full, attitude_design, source_design, phase, weight, resid, ids, start, segment)
    rows = ROWS // n_src
    field = pl.pallas_call(
        functools.partial(attitude_kernel, n_src, n_tm),
        out_shape=jax.ShapeDtypeStruct((4, 8, 128), f32),
        in_specs=vmem(1),
        out_specs=vmem(1)[0],
        scratch_shapes=[
            pltpu.VMEM((n_src - 1, n_tm, rows, 8, 128), f32),
            pltpu.VMEM((n_tm, rows, 8, 128), f32),
            pltpu.VMEM((n_tm - 1, rows, 8, 128), f32),
            pltpu.VMEM((ROWS, 8, 128), f32),
            pltpu.VMEM((2, ROWS, 128), f32),
            pltpu.VMEM((2, ROWS, 128), f32),
            pltpu.VMEM((ROWS, 16, 128), f32),
            pltpu.VMEM((ITERS, 2, 8, 128), f32),
            pltpu.VMEM((ITERS, n_tm - 1, 2, 8, 128), f32),
            pltpu.SemaphoreType.DMA((2, n_src - 1)),
            pltpu.SemaphoreType.DMA((2, n_tm - 1)),
            pltpu.SemaphoreType.DMA((2, n_src - 1)),
            pltpu.SemaphoreType.DMA((2, 2)),
            pltpu.SemaphoreType.DMA((2, ITERS * (n_tm - 1))),
        ],
        compiler_params=pltpu.CompilerParams(
            collective_id=1, has_side_effects=True, vmem_limit_bytes=56 * 1024 * 1024
        ),
    )(partial_band)
    return update, field.reshape(4, KS)


def solution(mesh):
    n_src, n_tm = mesh.shape["src"], mesh.shape["tm"]
    both = ("src", "tm")
    in_specs = (
        P(None, both),
        P(None, both),
        P(both),
        P(both),
        P(both),
        P(both),
        P(both),
        P(both, None),
    )
    out_specs = (P(None, "src"), P(None, "tm"))
    return jax.shard_map(
        functools.partial(body, n_src, n_tm),
        mesh=mesh,
        in_specs=in_specs,
        out_specs=out_specs,
        check_vma=False,
    )
```

time: 385 us -> 78.1 us (0.20)
  waiting for transfers between devices: 125 us -> 0 us
  Pallas kernels: 0 us -> 75.2 us
  blocking collectives: 74.9 us -> 0 us
  matrix products: 67.1 us -> 0 us
  local copies, waits for them, and re-layouts: 45.6 us -> 1.96 us
  starting transfers between devices: 27 us -> 0 us
  between operations: 23.2 us -> 0.65 us
  other arithmetic: 17.3 us -> 0 us
    psum x2 -> x0, waiting for transfers between devices: 91.9 us -> none  [the longest x1 55.2 us: body(): band = lax.psum(partial_band, 'src')]
    pallas_call x0 -> x4, Pallas kernels: none -> 75.2 us  [the longest x1 41.5 us: body(): pl.pallas_call(functools.partial(attitude_kernel, n_src, n_tm), out_shape...]
    psum x7 -> x0, blocking collectives: 74.9 us -> none  [the longest x4 39.3 us: squares(): return lax.psum(jnp.sum(resid * resid), 'tm')]
    dot_general x24 -> x0, matrix products: 67.1 us -> none  [the longest x16 51 us: add_block(): jnp.dot(feat, onehot, precision=lax.Precision.HIGHEST, preferred_element_...]
    another operation x6 -> x0, local copies, waits for them, and re-layouts: 32.3 us -> none  [the longest x3 24.5 us: knot_features(): return jnp.stack(rows, 0)]
    reduce_scatter x1 -> x0, waiting for transfers between devices: 29 us -> none  [body(): lax.psum_scatter(full_band, 'tm', scatter_dimension=1, tiled=True)]
    ppermute x9 -> x0, starting transfers between devices: 26.7 us -> none  [the longest x4 18.2 us: with_halo(): lax.ppermute(tail, axis, [(i, (i + 1) % count) for i in range(ends)])]
    dynamic_slice x24 -> x0, local copies, waits for them, and re-layouts: 5.92 us -> none  [collect(): lax.scan(add_block, jnp.zeros((width, count), jnp.float32), (feat_blocks,...]
  transfers between devices with their start and end apart: 12 -> 0, of which waited for: 7 -> 0; matrix products, arithmetic and copies ran while one was open for 1% -> 0% of each run, Pallas kernels for 0% -> 0%
where the time goes in v1:
time: 78.1 us; the launch traced here: 77.8 us
  Pallas kernels  75.2 us (96%)
  local copies, waits for them, and re-layouts  1.96 us (3%)
    pallas_call x1, Pallas kernels, body(): pl.pallas_call(functools.partial(attitude_kernel, n_src, n_tm), out_shape...  41.5 us
    pallas_call x1, Pallas kernels, body(): pl.pallas_call(functools.partial(normals_kernel, n_tm), out_shape=[jax.Sh...  16.3 us
    pallas_call x1, Pallas kernels, body(): pl.pallas_call(functools.partial(knot_kernel, n_tm), out_shape=jax.ShapeD...  14.7 us
    pallas_call x1, Pallas kernels, body(): pl.pallas_call(source_kernel, out_shape=jax.ShapeDtypeStruct((SRC_GROUPS,...  2.7 us
    unnamed x4, local copies, waits for them, and re-layouts  1.96 us

profile of v1, /device:TPU:0, one launch (start us, length us, event | category | flops | bytes accessed | tf_op | source)
XLA Modules:
  0.0 77.8 jit_solution(10544608273974333528)
XLA Ops:
  0.6 2.7 %shard_map.95.own_ref = f32[8,24,256]{2,1,0:T(8,128)} custom-call(f32[5,4096]{1,0:T(8,128)} %design_ref.3, f32[1,4096]{1,0:T(1,128)} %bitcast.10, f32[1,4096]{1,0:T(1,128)} %bitcast.12, s32[1,4096]{1,0:T(1,128)} %bitcast.14), custom_call_target="tpu_custom_call" | custom-call | tf_op jit(solution)/shard_map/pallas_call | solution.py:386
  3.3 16.3 %shard_map.96 = (f32[8,8,256]{2,1,0:T(8,128)}, f32[5,2048]{1,0:T(8,128)}) custom-call(f32[8,24,256]{2,1,0:T(8,128)} %shard_map.95.own_ref), custom_call_target="tpu_custom_call" | custom-call | tf_op jit(solution)/shard_map/pallas_call | solution.py:395
  19.7 14.7 %shard_map.97.part_ref = f32[4,48,8,128]{3,2,1,0:T(8,128)} custom-call(f32[8,8,256]{2,1,0:T(8,128)} %get-tuple-element.5.full_ref, f32[4,4096]{1,0:T(4,128)} %attitude_ref.1, f32[5,4096]{1,0:T(8,128)} %design_ref.3, f32[1,4096]{1,0:T(1,128)} %bitcast.17, f32[1,4096]{1,0:T(1,128)} %bitcast.11, f32[1,4096]{1,0:T(1,128)} %bitcast.13, s32[1,4096]{1,0:T(1,128)} %bitcast.15, ...), custom_call_target="tpu_custom_call" | custom-call | tf_op jit(solution)/shard_map/pallas_call | solution.py:411
  34.3 0.0 copy-start
  34.3 41.5 %shard_map.98 = f32[4,8,128]{2,1,0:T(8,128)} custom-call(f32[4,48,8,128]{3,2,1,0:T(8,128)} %shard_map.97.part_ref), custom_call_target="tpu_custom_call" | custom-call | tf_op jit(solution)/shard_map/pallas_call | solution.py:424
  75.9 1.3 %copy.12 = f32[1,4,8,128]{3,1,2,0:T(4,128)} copy(f32[1,4,8,128]{3,2,1,0:T(8,128)} %bitcast.16) | data formatting | bytes 32768
  77.2 0.0 copy-done
  77.2 0.6 copy.14
Async XLA Ops:
  34.3 42.9 %copy-start = (f32[5,2048]{1,0:T(8,128)S(1)}, f32[5,2048]{1,0:T(8,128)}, u32[]{:S(2)}) copy-start(f32[5,2048]{1,0:T(8,128)} %get-tuple-element.8) | copy-start | bytes 122884

commit v2 on v1

v2 whole, which is shorter than its diff:
```python
import functools

import jax
import jax.numpy as jnp
from jax import lax
from jax.experimental import pallas as pl
from jax.experimental.pallas import tpu as pltpu
from jax.sharding import PartitionSpec as P

KS = 1024
S_DEV = 2048
ITERS = 4
ROOMS = (40, 32, 24, 16)
FEATS = sum(ROOMS)
SRC_GROUPS = 8
SRC_WIDE = S_DEV // SRC_GROUPS
MESH = pl.DeviceIdType.MESH

prior_source = 1.0
prior_attitude = 1.0
index_pairs = [(i, j) for i in range(5) for j in range(i, 5)]
component_pairs = [(c, e) for c in range(4) for e in range(c, 4)]
NT = (((1,), (1,)), ((), ()))


def split(x):
    high = x.astype(jnp.bfloat16)
    low = (x - high.astype(jnp.float32)).astype(jnp.bfloat16)
    return high, low


def onehot(count, index, base):
    place = lax.broadcasted_iota(jnp.int32, (count, index.shape[1]), 0) + base
    return jnp.where(place == index, 1.0, 0.0).astype(jnp.bfloat16)


def solve_five(normals):
    entry = {}
    for n, (i, j) in enumerate(index_pairs):
        entry[j, i] = normals[n]
    for i in range(5):
        entry[i, i] = entry[i, i] + prior_source
    lower = {}
    for i in range(5):
        for j in range(i + 1):
            value = entry[i, j]
            for k in range(j):
                value = value - lower[i, k] * lower[j, k]
            if i == j:
                lower[i, i] = jnp.sqrt(value)
            else:
                lower[i, j] = value / lower[j, j]
    forward = []
    for i in range(5):
        value = normals[15 + i]
        for k in range(i):
            value = value - lower[i, k] * forward[k]
        forward.append(value / lower[i, i])
    result = [None] * 5
    for i in range(4, -1, -1):
        value = forward[i]
        for k in range(i + 1, 5):
            value = value - lower[k, i] * result[k]
        result[i] = value / lower[i, i]
    return result


def send(src, dst, sems, slot, peer):
    copy = pltpu.make_async_remote_copy(
        src_ref=src,
        dst_ref=dst,
        send_sem=sems.at[0, slot],
        recv_sem=sems.at[1, slot],
        device_id=peer,
        device_id_type=MESH,
    )
    copy.start()
    return copy


def shifted(x, by):
    lane = lax.broadcasted_iota(jnp.int32, x.shape, 2)
    turned = pltpu.roll(x, (128 - by) % 128, 2)
    if by > 0:
        return jnp.where(lane >= 128 - by, pltpu.roll(turned, 15, 1), turned)
    return jnp.where(lane < -by, pltpu.roll(turned, 1, 1), turned)


def source_sums(design, w, r, ids, lhs, own_ref):
    q = [design[i : i + 1, :] for i in range(5)]
    wq = [w * q[i] for i in range(5)]
    rows = [wq[i] * q[j] for i, j in index_pairs] + [wq[i] * r for i in range(5)]
    rows += [jnp.zeros_like(w)] * 4
    high, low = split(jnp.concatenate(rows, 0))
    both = jnp.concatenate([high.astype(jnp.float32), low.astype(jnp.float32)], 0)
    group = ids // SRC_WIDE
    for a in range(SRC_GROUPS):
        lhs[48 * a : 48 * a + 48, :] = jnp.where(group == a, both, 0.0).astype(jnp.bfloat16)
    hot = onehot(SRC_WIDE, ids % SRC_WIDE, 0)
    got = lax.dot_general(lhs[...], hot, NT, preferred_element_type=jnp.float32)
    for a in range(SRC_GROUPS):
        own_ref[a] = got[48 * a : 48 * a + 24] + got[48 * a + 24 : 48 * a + 48]


def behind(value, by, carried, lane):
    value = pltpu.roll(value, by, 1)
    front = 0.0 if carried is None else carried
    return value, jnp.where(lane < by, front, value)


def kernel(
    n_src, n_tm,
    attitude_ref, design_ref, phase_ref, weight_ref, resid_ref, id_ref, start_ref, segment_ref,
    update_ref, out_ref,
    own, landed, gathered, lhs_s, feat, lhs, acc, feat_r, lhs_r, acc_r,
    part, part_r, rs1, s1, rs2, full, rhs_in, rhs_all,
    stage, halo, ext, red, red_in,
    sem_n, sem_g, sem_a, sem_b, sem_c, sem_p, sem_q, sem_d, sem_e,
):
    me_s, me_t = lax.axis_index("src"), lax.axis_index("tm")
    n_obs = phase_ref.shape[1]
    side = [(lax.rem(me_s + o, n_src), me_t) for o in range(1, n_src)]
    line = [(me_s, lax.rem(me_t + o, n_tm)) for o in range(1, n_tm)]
    barrier = pltpu.get_barrier_semaphore()
    for peer in side + line:
        pl.semaphore_signal(barrier, inc=1, device_id=peer, device_id_type=MESH)

    w, ids = weight_ref[...], id_ref[...]
    source_sums(design_ref, w, resid_ref[...], ids, lhs_s, own)
    pl.semaphore_wait(barrier, len(side) + len(line))
    part_s = SRC_GROUPS // n_tm
    normals = []
    for o in range(1, n_tm):
        peer = line[o - 1]
        normals.append(
            send(own.at[pl.ds(peer[1] * part_s, part_s)], landed.at[o - 1], sem_n, o - 1, peer)
        )

    t = phase_ref[...]
    rest = 1.0 - t
    square = t * t
    cube = square * t
    basis = [
        rest * rest * rest / 6.0,
        (3.0 * cube - 6.0 * square + 4.0) / 6.0,
        (-3.0 * cube + 3.0 * square + 3.0 * t + 1.0) / 6.0,
        cube / 6.0,
    ]
    att = attitude_ref[...]
    outer = jnp.concatenate([att[c : c + 1] * att[e : e + 1] for c, e in component_pairs], 0)
    top = 0
    for j in range(4):
        scaled = w * basis[j]
        pieces = [outer * (scaled * basis[j + d]) for d in range(4 - j)]
        if ROOMS[j] > 40 - 10 * j:
            pieces.append(jnp.zeros((ROOMS[j] - 40 + 10 * j, n_obs), jnp.float32))
        high, low = split(jnp.concatenate(pieces, 0))
        feat[top : top + ROOMS[j], :] = high.astype(jnp.float32)
        feat[FEATS + top : FEATS + top + ROOMS[j], :] = low.astype(jnp.float32)
        top += ROOMS[j]
    segment, start = segment_ref[...], start_ref[...]
    tall = 2 * FEATS
    for s in range(n_tm):
        lhs[tall * s : tall * s + tall, :] = jnp.where(segment == s, feat[...], 0.0).astype(
            jnp.bfloat16
        )

    def tile(n, carry):
        knots = onehot(256, start, n * 256)
        place = pl.ds(pl.multiple_of(n * 256, 256), 256)
        acc[:, place] = lax.dot_general(lhs[...], knots, NT, preferred_element_type=jnp.float32)
        return carry

    tiles = KS // 256
    lax.fori_loop(0, tiles // 2, tile, 0)

    mine = pl.ds(me_t * part_s, part_s)
    total = own[mine]
    for o in range(1, n_tm):
        normals[o - 1].wait_recv()
        total = total + landed[o - 1]
    solved = solve_five([total[:, n, :] for n in range(20)])
    for g in range(part_s):
        for i in range(5):
            gathered[me_t * part_s + g, i : i + 1, :] = solved[i][g : g + 1, :]
        gathered[me_t * part_s + g, 5:8, :] = jnp.zeros((3, SRC_WIDE), jnp.float32)
    gathers = []
    for o in range(1, n_tm):
        gathers.append(send(gathered.at[mine], gathered.at[mine], sem_g, o - 1, line[o - 1]))

    lax.fori_loop(tiles // 2, tiles, tile, 0)

    lane = lax.broadcasted_iota(jnp.int32, (1, KS), 1)
    rows_all = part.shape[1]
    before = [None] * 4
    for s in range(n_tm):
        total = None
        top = tall * s
        for j in range(4):
            room, size = ROOMS[j], 40 - 10 * j
            value = acc[top : top + room, :] + acc[FEATS + top : FEATS + top + room, :]
            top += room
            if j == 0:
                total = value
                continue
            before[j], value = behind(value, j, before[j], lane)
            total = total + jnp.concatenate([value, jnp.zeros((40 - room, KS), jnp.float32)], 0)
        part[s, 0:40] = total.reshape(40, 8, 128)
        if rows_all > 40:
            part[s, 40:rows_all] = jnp.zeros((rows_all - 40, 8, 128), jnp.float32)
    rows = rows_all // n_src
    first = []
    for o in range(1, n_src):
        peer = side[o - 1]
        first.append(
            send(part.at[:, pl.ds(peer[0] * rows, rows)], rs1.at[o - 1], sem_a, o - 1, peer)
        )

    for copy in gathers:
        copy.wait()
    for copy in normals:
        copy.wait_send()
    for a in range(SRC_GROUPS):
        update_ref[:, a * SRC_WIDE : (a + 1) * SRC_WIDE] = gathered[a, 0:5]
    group = ids // SRC_WIDE
    hot = onehot(SRC_WIDE, ids % SRC_WIDE, 0)
    high, low = split(gathered[...].reshape(SRC_GROUPS * 8, SRC_WIDE))
    picks = jnp.dot(high, hot, preferred_element_type=jnp.float32) + jnp.dot(
        low, hot, preferred_element_type=jnp.float32
    )
    picked = jnp.zeros((8, n_obs), jnp.float32)
    for a in range(SRC_GROUPS):
        picked = picked + jnp.where(group == a, picks[8 * a : 8 * a + 8], 0.0)
    fitted = jnp.sum(design_ref[...] * picked[0:5], axis=0, keepdims=True)
    weighted = w * (resid_ref[...] - fitted)
    high, low = split(jnp.concatenate([att * (weighted * basis[j]) for j in range(4)], 0))
    feat_r[0:16, :] = high.astype(jnp.float32)
    feat_r[16:32, :] = low.astype(jnp.float32)
    for s in range(n_tm):
        lhs_r[32 * s : 32 * s + 32, :] = jnp.where(segment == s, feat_r[...], 0.0).astype(
            jnp.bfloat16
        )

    def tile_r(n, carry):
        knots = onehot(256, start, n * 256)
        place = pl.ds(pl.multiple_of(n * 256, 256), 256)
        acc_r[:, place] = lax.dot_general(lhs_r[...], knots, NT, preferred_element_type=jnp.float32)
        return carry

    lax.fori_loop(0, tiles, tile_r, 0)
    before = [None] * 4
    for s in range(n_tm):
        total = None
        for j in range(4):
            top = 32 * s + 4 * j
            value = acc_r[top : top + 4, :] + acc_r[16 + top : 20 + top, :]
            if j == 0:
                total = value
                continue
            before[j], value = behind(value, j, before[j], lane)
            total = total + value
        part_r[s] = total.reshape(4, 8, 128)

    rhs_first = []
    for o in range(1, n_tm):
        peer = line[o - 1]
        rhs_first.append(send(part_r.at[peer[1]], rhs_in.at[o - 1], sem_p, o - 1, peer))
    own_rows = pl.ds(me_s * rows, rows)
    total = part[:, own_rows]
    for o in range(1, n_src):
        first[o - 1].wait_recv()
        total = total + rs1[o - 1]
    s1[...] = total
    second = []
    for o in range(1, n_tm):
        peer = line[o - 1]
        second.append(send(s1.at[peer[1]], rs2.at[o - 1], sem_b, o - 1, peer))

    total = part_r[me_t]
    for o in range(1, n_tm):
        rhs_first[o - 1].wait_recv()
        total = total + rhs_in[o - 1]
    rhs_all[me_s] = total
    rhs_second = []
    for o in range(1, n_src):
        rhs_second.append(send(rhs_all.at[me_s], rhs_all.at[me_s], sem_q, o - 1, side[o - 1]))
    total = s1[me_t]
    for o in range(1, n_tm):
        second[o - 1].wait_recv()
        total = total + rs2[o - 1]
    full[own_rows] = total
    third = []
    for o in range(1, n_src):
        third.append(send(full.at[own_rows], full.at[own_rows], sem_c, o - 1, side[o - 1]))
    for copy in first + second + rhs_first:
        copy.wait_send()
    for copy in rhs_second:
        copy.wait()
    rhs = rhs_all[0]
    for s in range(1, n_src):
        rhs = rhs + rhs_all[s]
    for copy in third:
        copy.wait()

    whole = jnp.concatenate([rhs, full[0:40]], 0)
    stage[0] = whole[:, 0, :]
    stage[1] = whole[:, 7, :]
    to_behind = send(stage.at[0], halo.at[0], sem_d, 0, line[n_tm - 2])
    to_ahead = send(stage.at[1], halo.at[1], sem_d, 1, line[0])
    ext[:, 0:8, :] = whole
    ext[:, 8:16, :] = jnp.zeros((44, 8, 128), jnp.float32)
    to_behind.wait()
    to_ahead.wait()
    ext[:, 8, :] = halo[0] * jnp.where(me_t < n_tm - 1, 1.0, 0.0)
    ext[:, 15, :] = halo[1] * jnp.where(me_t > 0, 1.0, 0.0)

    row = lax.broadcasted_iota(jnp.int32, (1, 16, 128), 1)
    kept = jnp.where(row < 8, 1.0, 0.0)
    kept = kept + jnp.where(row == 8, 1.0, 0.0) * jnp.where(me_t < n_tm - 1, 1.0, 0.0)
    kept = kept + jnp.where(row == 15, 1.0, 0.0) * jnp.where(me_t > 0, 1.0, 0.0)
    columns = []
    for d in range(4):
        for e in range(4):
            columns.append(
                jnp.stack(
                    [
                        ext[4 + 10 * d + component_pairs.index((min(c, e), max(c, e)))]
                        for c in range(4)
                    ],
                    0,
                )
            )

    def multiply(d, x):
        value = columns[4 * d] * x[0:1]
        for e in range(1, 4):
            value = value + columns[4 * d + e] * x[e : e + 1]
        return value

    def image_of(x):
        value = prior_attitude * x + multiply(0, x)
        for d in range(1, 4):
            value = value + multiply(d, shifted(x, d)) + shifted(multiply(d, x), -d)
        return value * kept

    resid = ext[0:4]
    direction = resid
    field = None
    image = None
    alpha = None
    gamma_old = None
    for step in range(ITERS):
        applied = image_of(resid)
        inner = resid[:, 0:8, :]
        red[step, 0] = jnp.sum(inner * inner, axis=0)
        red[step, 1] = jnp.sum(inner * applied[:, 0:8, :], axis=0)
        sums = []
        for o in range(1, n_tm):
            sums.append(
                send(red.at[step], red_in.at[step, o - 1], sem_e, step * (n_tm - 1) + o - 1, line[o - 1])
            )
        value = red[step]
        for o in range(1, n_tm):
            sums[o - 1].wait()
            value = value + red_in[step, o - 1]
        gamma = jnp.sum(value[0:1], axis=(1, 2), keepdims=True)
        delta = jnp.sum(value[1:2], axis=(1, 2), keepdims=True)
        if step == 0:
            alpha = gamma / delta
            direction, image = resid, applied
            field = alpha * direction
        else:
            beta = gamma / gamma_old
            alpha = gamma / (delta - beta * (gamma / alpha))
            direction = resid + beta * direction
            image = applied + beta * image
            field = field + alpha * direction
        resid = resid - alpha * image
        gamma_old = gamma
    for k in range(8):
        out_ref[:, 128 * k : 128 * k + 128] = field[:, k, :]


def body(
    n_src,
    n_tm,
    attitude_design,
    source_design,
    scan_phase,
    obs_weight,
    obs_residual,
    source_id,
    knot_start,
    time_segment,
):
    n_obs = scan_phase.shape[0]
    f32, bf16 = jnp.float32, jnp.bfloat16
    flat = lambda x: x.reshape(1, n_obs)
    rows_all = -(-40 // n_src) * n_src
    rows = rows_all // n_src
    part_s = SRC_GROUPS // n_tm
    sems = lambda count: pltpu.SemaphoreType.DMA((2, count))
    update, field = pl.pallas_call(
        functools.partial(kernel, n_src, n_tm),
        out_shape=[jax.ShapeDtypeStruct((5, S_DEV), f32), jax.ShapeDtypeStruct((4, KS), f32)],
        in_specs=[pl.BlockSpec(memory_space=pltpu.VMEM)] * 8,
        out_specs=[pl.BlockSpec(memory_space=pltpu.VMEM)] * 2,
        scratch_shapes=[
            pltpu.VMEM((SRC_GROUPS, 24, SRC_WIDE), f32),
            pltpu.VMEM((n_tm - 1, part_s, 24, SRC_WIDE), f32),
            pltpu.VMEM((SRC_GROUPS, 8, SRC_WIDE), f32),
            pltpu.VMEM((48 * SRC_GROUPS, n_obs), bf16),
            pltpu.VMEM((2 * FEATS, n_obs), f32),
            pltpu.VMEM((2 * FEATS * n_tm, n_obs), bf16),
            pltpu.VMEM((2 * FEATS * n_tm, KS), f32),
            pltpu.VMEM((32, n_obs), f32),
            pltpu.VMEM((32 * n_tm, n_obs), bf16),
            pltpu.VMEM((32 * n_tm, KS), f32),
            pltpu.VMEM((n_tm, rows_all, 8, 128), f32),
            pltpu.VMEM((n_tm, 4, 8, 128), f32),
            pltpu.VMEM((n_src - 1, n_tm, rows, 8, 128), f32),
            pltpu.VMEM((n_tm, rows, 8, 128), f32),
            pltpu.VMEM((n_tm - 1, rows, 8, 128), f32),
            pltpu.VMEM((rows_all, 8, 128), f32),
            pltpu.VMEM((n_tm - 1, 4, 8, 128), f32),
            pltpu.VMEM((n_src, 4, 8, 128), f32),
            pltpu.VMEM((2, 44, 128), f32),
            pltpu.VMEM((2, 44, 128), f32),
            pltpu.VMEM((44, 16, 128), f32),
            pltpu.VMEM((ITERS, 2, 8, 128), f32),
            pltpu.VMEM((ITERS, n_tm - 1, 2, 8, 128), f32),
            sems(n_tm - 1),
            sems(n_tm - 1),
            sems(n_src - 1),
            sems(n_tm - 1),
            sems(n_src - 1),
            sems(n_tm - 1),
            sems(n_src - 1),
            sems(2),
            sems(ITERS * (n_tm - 1)),
        ],
        compiler_params=pltpu.CompilerParams(
            collective_id=0, has_side_effects=True, vmem_limit_bytes=56 * 1024 * 1024
        ),
    )(
        attitude_design,
        source_design,
        flat(scan_phase),
        flat(obs_weight),
        flat(obs_residual),
        flat(source_id),
        flat(knot_start),
        flat(time_segment),
    )
    return update, field


def solution(mesh):
    n_src, n_tm = mesh.shape["src"], mesh.shape["tm"]
    both = ("src", "tm")
    in_specs = (
        P(None, both),
        P(None, both),
        P(both),
        P(both),
        P(both),
        P(both),
        P(both),
        P(both, None),
    )
    out_specs = (P(None, "src"), P(None, "tm"))
    return jax.shard_map(
        functools.partial(body, n_src, n_tm),
        mesh=mesh,
        in_specs=in_specs,
        out_specs=out_specs,
        check_vma=False,
    )
```

time: 78.1 us -> 57.2 us (0.73)
  Pallas kernels: 75.2 us -> 54.3 us
    pallas_call x4 -> x1, Pallas kernels: 75.2 us -> 54.3 us  [body(): pl.pallas_call(functools.partial(kernel, n_src, n_tm), out_shape=[jax.Sha...]
where the time goes in v2:
time: 57.2 us; the launch traced here: 57 us
  Pallas kernels  54.3 us (95%)
  local copies, waits for them, and re-layouts  2.09 us (4%)
  between operations  0.65 us (1%)
    pallas_call x1, Pallas kernels, body(): pl.pallas_call(functools.partial(kernel, n_src, n_tm), out_shape=[jax.Sha...  54.3 us
    unnamed x4, local copies, waits for them, and re-layouts  2.09 us

profile of v2, /device:TPU:0, one launch (start us, length us, event | category | flops | bytes accessed | tf_op | source)
XLA Modules:
  0.0 57.0 jit_solution(7032162979789272232)
XLA Ops:
  0.6 54.3 %shard_map.95 = (f32[5,2048]{1,0:T(8,128)}, f32[4,1024]{1,0:T(4,128)}) custom-call(f32[4,4096]{1,0:T(4,128)} %attitude_ref.1, f32[5,4096]{1,0:T(8,128)} %design_ref.1, f32[1,4096]{1,0:T(1,128)} %bitcast.6, f32[1,4096]{1,0:T(1,128)} %bitcast.7, f32[1,4096]{1,0:T(1,128)} %bitcast.8, s32[1,4096]{1,0:T(1,128)} %bitcast.9, s32[1,4096]{1,0:T(1,128)} %bitcast.10, ...), custom_call_target="tpu_custom_call" | custom-call | tf_op jit(solution)/shard_map/pallas_call | solution.py:403
  54.9 0.0 copy-start
  54.9 1.5 %copy.12 = f32[5,2048]{1,0:T(8,128)} copy(f32[5,2048]{1,0:T(8,128)} %get-tuple-element.4) | data formatting | bytes 81920
  56.4 0.0 copy-done
  56.4 0.6 %copy.13 = f32[4,1024]{1,0:T(4,128)} copy(f32[4,1024]{1,0:T(4,128)S(1)} %copy-done) | data formatting | bytes 32768
Async XLA Ops:
  54.9 1.5 %copy-start = (f32[4,1024]{1,0:T(4,128)S(1)}, f32[4,1024]{1,0:T(4,128)}, u32[]{:S(2)}) copy-start(f32[4,1024]{1,0:T(4,128)} %get-tuple-element.5) | copy-start | bytes 49156

commit v3 on v2

--- a/solution.py
+++ b/solution.py
@@ -82,7 +82,7 @@
     lane = lax.broadcasted_iota(jnp.int32, x.shape, 2)
     turned = pltpu.roll(x, (128 - by) % 128, 2)
     if by > 0:
-        return jnp.where(lane >= 128 - by, pltpu.roll(turned, 15, 1), turned)
+        return jnp.where(lane >= 128 - by, pltpu.roll(turned, x.shape[1] - 1, 1), turned)
     return jnp.where(lane < -by, pltpu.roll(turned, 1, 1), turned)
 
 
@@ -113,8 +113,7 @@
     attitude_ref, design_ref, phase_ref, weight_ref, resid_ref, id_ref, start_ref, segment_ref,
     update_ref, out_ref,
     own, landed, gathered, lhs_s, feat, lhs, acc, feat_r, lhs_r, acc_r,
-    part, part_r, rs1, s1, rs2, full, rhs_in, rhs_all,
-    stage, halo, ext, red, red_in,
+    part, part_r, rs1, s1, rs2, segs, full, rhs_in, rhs_all, rhs_full, found,
     sem_n, sem_g, sem_a, sem_b, sem_c, sem_p, sem_q, sem_d, sem_e,
 ):
     me_s, me_t = lax.axis_index("src"), lax.axis_index("tm")
@@ -247,7 +246,18 @@
         acc_r[:, place] = lax.dot_general(lhs_r[...], knots, NT, preferred_element_type=jnp.float32)
         return carry
 
-    lax.fori_loop(0, tiles, tile_r, 0)
+    lax.fori_loop(0, tiles // 2, tile_r, 0)
+    own_rows = pl.ds(me_s * rows, rows)
+    total = part[:, own_rows]
+    for o in range(1, n_src):
+        first[o - 1].wait_recv()
+        total = total + rs1[o - 1]
+    s1[...] = total
+    second = []
+    for o in range(1, n_tm):
+        peer = line[o - 1]
+        second.append(send(s1.at[peer[1]], rs2.at[o - 1], sem_b, o - 1, peer))
+    lax.fori_loop(tiles // 2, tiles, tile_r, 0)
     before = [None] * 4
     for s in range(n_tm):
         total = None
@@ -265,16 +275,14 @@
     for o in range(1, n_tm):
         peer = line[o - 1]
         rhs_first.append(send(part_r.at[peer[1]], rhs_in.at[o - 1], sem_p, o - 1, peer))
-    own_rows = pl.ds(me_s * rows, rows)
-    total = part[:, own_rows]
-    for o in range(1, n_src):
-        first[o - 1].wait_recv()
-        total = total + rs1[o - 1]
-    s1[...] = total
-    second = []
-    for o in range(1, n_tm):
-        peer = line[o - 1]
-        second.append(send(s1.at[peer[1]], rs2.at[o - 1], sem_b, o - 1, peer))
+    total = s1[me_t]
+    for o in range(1, n_tm):
+        second[o - 1].wait_recv()
+        total = total + rs2[o - 1]
+    segs[me_t] = total
+    spread = []
+    for o in range(1, n_tm):
+        spread.append(send(segs.at[me_t], segs.at[me_t], sem_d, o - 1, line[o - 1]))
 
     total = part_r[me_t]
     for o in range(1, n_tm):
@@ -284,50 +292,42 @@
     rhs_second = []
     for o in range(1, n_src):
         rhs_second.append(send(rhs_all.at[me_s], rhs_all.at[me_s], sem_q, o - 1, side[o - 1]))
-    total = s1[me_t]
-    for o in range(1, n_tm):
-        second[o - 1].wait_recv()
-        total = total + rs2[o - 1]
-    full[own_rows] = total
+    for copy in spread:
+        copy.wait()
     third = []
     for o in range(1, n_src):
-        third.append(send(full.at[own_rows], full.at[own_rows], sem_c, o - 1, side[o - 1]))
-    for copy in first + second + rhs_first:
-        copy.wait_send()
+        third.append(send(segs, full.at[me_s], sem_c, o - 1, side[o - 1]))
+    full[me_s] = segs[...]
     for copy in rhs_second:
         copy.wait()
     rhs = rhs_all[0]
     for s in range(1, n_src):
         rhs = rhs + rhs_all[s]
+    rhs_full[me_t] = rhs
+    rhs_third = []
+    for o in range(1, n_tm):
+        rhs_third.append(send(rhs_full.at[me_t], rhs_full.at[me_t], sem_e, o - 1, line[o - 1]))
+    for copy in first + second + rhs_first:
+        copy.wait_send()
+    for copy in rhs_third:
+        copy.wait()
     for copy in third:
         copy.wait()
 
-    whole = jnp.concatenate([rhs, full[0:40]], 0)
-    stage[0] = whole[:, 0, :]
-    stage[1] = whole[:, 7, :]
-    to_behind = send(stage.at[0], halo.at[0], sem_d, 0, line[n_tm - 2])
-    to_ahead = send(stage.at[1], halo.at[1], sem_d, 1, line[0])
-    ext[:, 0:8, :] = whole
-    ext[:, 8:16, :] = jnp.zeros((44, 8, 128), jnp.float32)
-    to_behind.wait()
-    to_ahead.wait()
-    ext[:, 8, :] = halo[0] * jnp.where(me_t < n_tm - 1, 1.0, 0.0)
-    ext[:, 15, :] = halo[1] * jnp.where(me_t > 0, 1.0, 0.0)
-
-    row = lax.broadcasted_iota(jnp.int32, (1, 16, 128), 1)
-    kept = jnp.where(row < 8, 1.0, 0.0)
-    kept = kept + jnp.where(row == 8, 1.0, 0.0) * jnp.where(me_t < n_tm - 1, 1.0, 0.0)
-    kept = kept + jnp.where(row == 15, 1.0, 0.0) * jnp.where(me_t > 0, 1.0, 0.0)
+    tall = 8 * n_tm
+    knot = lax.broadcasted_iota(jnp.int32, (tall, 128), 0) * 128
+    knot = knot + lax.broadcasted_iota(jnp.int32, (tall, 128), 1)
     columns = []
     for d in range(4):
+        bands = []
+        for q in range(10):
+            place = 10 * d + q
+            band = full[place // rows, :, place % rows].reshape(tall, 128)
+            bands.append(band if d == 0 else jnp.where(knot < tall * 128 - d, band, 0.0))
         for e in range(4):
             columns.append(
                 jnp.stack(
-                    [
-                        ext[4 + 10 * d + component_pairs.index((min(c, e), max(c, e)))]
-                        for c in range(4)
-                    ],
-                    0,
+                    [bands[component_pairs.index((min(c, e), max(c, e)))] for c in range(4)], 0
                 )
             )
 
@@ -341,44 +341,29 @@
         value = prior_attitude * x + multiply(0, x)
         for d in range(1, 4):
             value = value + multiply(d, shifted(x, d)) + shifted(multiply(d, x), -d)
-        return value * kept
-
-    resid = ext[0:4]
+        return value
+
+    def inner(x, y):
+        lanes = jnp.sum(x * y, axis=(0, 1), keepdims=True)
+        return jnp.sum(lanes, axis=2, keepdims=True)
+
+    resid = jnp.stack([rhs_full[:, c].reshape(tall, 128) for c in range(4)], 0)
     direction = resid
-    field = None
-    image = None
-    alpha = None
-    gamma_old = None
+    field = jnp.zeros_like(resid)
+    norm_now = inner(resid, resid)
     for step in range(ITERS):
-        applied = image_of(resid)
-        inner = resid[:, 0:8, :]
-        red[step, 0] = jnp.sum(inner * inner, axis=0)
-        red[step, 1] = jnp.sum(inner * applied[:, 0:8, :], axis=0)
-        sums = []
-        for o in range(1, n_tm):
-            sums.append(
-                send(red.at[step], red_in.at[step, o - 1], sem_e, step * (n_tm - 1) + o - 1, line[o - 1])
-            )
-        value = red[step]
-        for o in range(1, n_tm):
-            sums[o - 1].wait()
-            value = value + red_in[step, o - 1]
-        gamma = jnp.sum(value[0:1], axis=(1, 2), keepdims=True)
-        delta = jnp.sum(value[1:2], axis=(1, 2), keepdims=True)
-        if step == 0:
-            alpha = gamma / delta
-            direction, image = resid, applied
-            field = alpha * direction
-        else:
-            beta = gamma / gamma_old
-            alpha = gamma / (delta - beta * (gamma / alpha))
-            direction = resid + beta * direction
-            image = applied + beta * image
-            field = field + alpha * direction
-        resid = resid - alpha * image
-        gamma_old = gamma
+        image = image_of(direction)
+        alpha = norm_now / inner(direction, image)
+        field = field + alpha * direction
+        if step < ITERS - 1:
+            resid = resid - alpha * image
+            norm_next = inner(resid, resid)
+            direction = resid + norm_next / norm_now * direction
+            norm_now = norm_next
+    found[...] = field.reshape(4, n_tm, 8, 128)
+    mine = found[:, me_t]
     for k in range(8):
-        out_ref[:, 128 * k : 128 * k + 128] = field[:, k, :]
+        out_ref[:, 128 * k : 128 * k + 128] = mine[:, k, :]
 
 
 def body(
@@ -421,14 +406,12 @@
             pltpu.VMEM((n_src - 1, n_tm, rows, 8, 128), f32),
             pltpu.VMEM((n_tm, rows, 8, 128), f32),
             pltpu.VMEM((n_tm - 1, rows, 8, 128), f32),
-            pltpu.VMEM((rows_all, 8, 128), f32),
+            pltpu.VMEM((n_tm, rows, 8, 128), f32),
+            pltpu.VMEM((n_src, n_tm, rows, 8, 128), f32),
             pltpu.VMEM((n_tm - 1, 4, 8, 128), f32),
             pltpu.VMEM((n_src, 4, 8, 128), f32),
-            pltpu.VMEM((2, 44, 128), f32),
-            pltpu.VMEM((2, 44, 128), f32),
-            pltpu.VMEM((44, 16, 128), f32),
-            pltpu.VMEM((ITERS, 2, 8, 128), f32),
-            pltpu.VMEM((ITERS, n_tm - 1, 2, 8, 128), f32),
+            pltpu.VMEM((n_tm, 4, 8, 128), f32),
+            pltpu.VMEM((4, n_tm, 8, 128), f32),
             sems(n_tm - 1),
             sems(n_tm - 1),
             sems(n_src - 1),
@@ -436,8 +419,8 @@
             sems(n_src - 1),
             sems(n_tm - 1),
             sems(n_src - 1),
-            sems(2),
-            sems(ITERS * (n_tm - 1)),
+            sems(n_tm - 1),
+            sems(n_tm - 1),
         ],
         compiler_params=pltpu.CompilerParams(
             collective_id=0, has_side_effects=True, vmem_limit_bytes=56 * 1024 * 1024

time: 57.2 us -> 46.8 us (0.82)
  Pallas kernels: 54.3 us -> 43.6 us
    pallas_call x1, Pallas kernels: 54.3 us -> 43.6 us  [body(): pl.pallas_call(functools.partial(kernel, n_src, n_tm), out_shape=[jax.Sha...]
where the time goes in v3:
time: 46.8 us; the launch traced here: 46.4 us
  Pallas kernels  43.6 us (93%)
  local copies, waits for them, and re-layouts  2.09 us (4%)
  between operations  0.65 us (1%)
    pallas_call x1, Pallas kernels, body(): pl.pallas_call(functools.partial(kernel, n_src, n_tm), out_shape=[jax.Sha...  43.6 us
    unnamed x4, local copies, waits for them, and re-layouts  2.09 us

profile of v3, /device:TPU:0, one launch (start us, length us, event | category | flops | bytes accessed | tf_op | source)
XLA Modules:
  0.0 46.4 jit_solution(3735235566871192585)
XLA Ops:
  0.6 43.6 %shard_map.95 = (f32[5,2048]{1,0:T(8,128)}, f32[4,1024]{1,0:T(4,128)}) custom-call(f32[4,4096]{1,0:T(4,128)} %attitude_ref.1, f32[5,4096]{1,0:T(8,128)} %design_ref.1, f32[1,4096]{1,0:T(1,128)} %bitcast.6, f32[1,4096]{1,0:T(1,128)} %bitcast.7, f32[1,4096]{1,0:T(1,128)} %bitcast.8, s32[1,4096]{1,0:T(1,128)} %bitcast.9, s32[1,4096]{1,0:T(1,128)} %bitcast.10, ...), custom_call_target="tpu_custom_call" | custom-call | tf_op jit(solution)/shard_map/pallas_call | solution.py:388
  44.3 0.0 copy-start
  44.3 1.5 %copy.12 = f32[5,2048]{1,0:T(8,128)} copy(f32[5,2048]{1,0:T(8,128)} %get-tuple-element.4) | data formatting | bytes 81920
  45.8 0.0 copy-done
  45.8 0.6 %copy.13 = f32[4,1024]{1,0:T(4,128)} copy(f32[4,1024]{1,0:T(4,128)S(1)} %copy-done) | data formatting | bytes 32768
Async XLA Ops:
  44.3 1.5 %copy-start = (f32[4,1024]{1,0:T(4,128)S(1)}, f32[4,1024]{1,0:T(4,128)}, u32[]{:S(2)}) copy-start(f32[4,1024]{1,0:T(4,128)} %get-tuple-element.5) | copy-start | bytes 49156

commit v4 on v3

--- a/solution.py
+++ b/solution.py
@@ -159,19 +159,59 @@
         top += ROOMS[j]
     segment, start = segment_ref[...], start_ref[...]
     tall = 2 * FEATS
-    for s in range(n_tm):
-        lhs[tall * s : tall * s + tall, :] = jnp.where(segment == s, feat[...], 0.0).astype(
-            jnp.bfloat16
-        )
-
-    def tile(n, carry):
-        knots = onehot(256, start, n * 256)
-        place = pl.ds(pl.multiple_of(n * 256, 256), 256)
-        acc[:, place] = lax.dot_general(lhs[...], knots, NT, preferred_element_type=jnp.float32)
-        return carry
-
     tiles = KS // 256
-    lax.fori_loop(0, tiles // 2, tile, 0)
+    half = n_tm // 2
+    lane = lax.broadcasted_iota(jnp.int32, (1, KS), 1)
+    rows_all = part.shape[1]
+    rows = rows_all // n_src
+    before = [None] * 4
+    first = []
+
+    def band_half(begin):
+        for s in range(begin, begin + half):
+            lhs[tall * s : tall * s + tall, :] = jnp.where(segment == s, feat[...], 0.0).astype(
+                jnp.bfloat16
+            )
+        low_row, high_row = tall * begin, tall * (begin + half)
+
+        def tile(n, carry):
+            knots = onehot(256, start, n * 256)
+            place = pl.ds(pl.multiple_of(n * 256, 256), 256)
+            acc[low_row:high_row, place] = lax.dot_general(
+                lhs[low_row:high_row, :], knots, NT, preferred_element_type=jnp.float32
+            )
+            return carry
+
+        lax.fori_loop(0, tiles, tile, 0)
+        for s in range(begin, begin + half):
+            total = None
+            top = tall * s
+            for j in range(4):
+                room = ROOMS[j]
+                value = acc[top : top + room, :] + acc[FEATS + top : FEATS + top + room, :]
+                top += room
+                if j == 0:
+                    total = value
+                    continue
+                before[j], value = behind(value, j, before[j], lane)
+                total = total + jnp.concatenate([value, jnp.zeros((40 - room, KS), jnp.float32)], 0)
+            part[s, 0:40] = total.reshape(40, 8, 128)
+            if rows_all > 40:
+                part[s, 40:rows_all] = jnp.zeros((rows_all - 40, 8, 128), jnp.float32)
+        some = pl.ds(begin, half)
+        for o in range(1, n_src):
+            peer = side[o - 1]
+            first.append(
+                send(
+                    part.at[some, pl.ds(peer[0] * rows, rows)],
+                    rs1.at[o - 1, some],
+                    sem_a,
+                    len(first),
+                    peer,
+                )
+            )
+
+    band_half(0)
 
     mine = pl.ds(me_t * part_s, part_s)
     total = own[mine]
@@ -187,33 +227,7 @@
     for o in range(1, n_tm):
         gathers.append(send(gathered.at[mine], gathered.at[mine], sem_g, o - 1, line[o - 1]))
 
-    lax.fori_loop(tiles // 2, tiles, tile, 0)
-
-    lane = lax.broadcasted_iota(jnp.int32, (1, KS), 1)
-    rows_all = part.shape[1]
-    before = [None] * 4
-    for s in range(n_tm):
-        total = None
-        top = tall * s
-        for j in range(4):
-            room, size = ROOMS[j], 40 - 10 * j
-            value = acc[top : top + room, :] + acc[FEATS + top : FEATS + top + room, :]
-            top += room
-            if j == 0:
-                total = value
-                continue
-            before[j], value = behind(value, j, before[j], lane)
-            total = total + jnp.concatenate([value, jnp.zeros((40 - room, KS), jnp.float32)], 0)
-        part[s, 0:40] = total.reshape(40, 8, 128)
-        if rows_all > 40:
-            part[s, 40:rows_all] = jnp.zeros((rows_all - 40, 8, 128), jnp.float32)
-    rows = rows_all // n_src
-    first = []
-    for o in range(1, n_src):
-        peer = side[o - 1]
-        first.append(
-            send(part.at[:, pl.ds(peer[0] * rows, rows)], rs1.at[o - 1], sem_a, o - 1, peer)
-        )
+    band_half(half)
 
     for copy in gathers:
         copy.wait()
@@ -251,6 +265,7 @@
     total = part[:, own_rows]
     for o in range(1, n_src):
         first[o - 1].wait_recv()
+        first[n_src - 1 + o - 1].wait_recv()
         total = total + rs1[o - 1]
     s1[...] = total
     second = []
@@ -280,10 +295,17 @@
         second[o - 1].wait_recv()
         total = total + rs2[o - 1]
     segs[me_t] = total
+    third = []
+
+    def pass_on(slot):
+        for peer in side:
+            third.append(send(segs.at[slot], full.at[me_s, slot], sem_c, len(third), peer))
+
     spread = []
     for o in range(1, n_tm):
         spread.append(send(segs.at[me_t], segs.at[me_t], sem_d, o - 1, line[o - 1]))
 
+    pass_on(me_t)
     total = part_r[me_t]
     for o in range(1, n_tm):
         rhs_first[o - 1].wait_recv()
@@ -292,11 +314,9 @@
     rhs_second = []
     for o in range(1, n_src):
         rhs_second.append(send(rhs_all.at[me_s], rhs_all.at[me_s], sem_q, o - 1, side[o - 1]))
-    for copy in spread:
-        copy.wait()
-    third = []
-    for o in range(1, n_src):
-        third.append(send(segs, full.at[me_s], sem_c, o - 1, side[o - 1]))
+    for o in range(1, n_tm):
+        spread[o - 1].wait_recv()
+        pass_on(lax.rem(me_t + n_tm - o, n_tm))
     full[me_s] = segs[...]
     for copy in rhs_second:
         copy.wait()
@@ -307,7 +327,7 @@
     rhs_third = []
     for o in range(1, n_tm):
         rhs_third.append(send(rhs_full.at[me_t], rhs_full.at[me_t], sem_e, o - 1, line[o - 1]))
-    for copy in first + second + rhs_first:
+    for copy in first + second + rhs_first + spread:
         copy.wait_send()
     for copy in rhs_third:
         copy.wait()
@@ -414,9 +434,9 @@
             pltpu.VMEM((4, n_tm, 8, 128), f32),
             sems(n_tm - 1),
             sems(n_tm - 1),
-            sems(n_src - 1),
-            sems(n_tm - 1),
-            sems(n_src - 1),
+            sems(2 * (n_src - 1)),
+            sems(n_tm - 1),
+            sems(n_tm * (n_src - 1)),
             sems(n_tm - 1),
             sems(n_src - 1),
             sems(n_tm - 1),

time: 46.8 us -> 44.3 us (0.947)
  Pallas kernels: 43.6 us -> 41.4 us
    pallas_call x1, Pallas kernels: 43.6 us -> 41.4 us  [body(): pl.pallas_call(functools.partial(kernel, n_src, n_tm), out_shape=[jax.Sha...]
where the time goes in v4:
time: 44.3 us; the launch traced here: 44.1 us
  Pallas kernels  41.4 us (93%)
  local copies, waits for them, and re-layouts  2.09 us (5%)
  between operations  0.65 us (1%)
    pallas_call x1, Pallas kernels, body(): pl.pallas_call(functools.partial(kernel, n_src, n_tm), out_shape=[jax.Sha...  41.4 us
    unnamed x4, local copies, waits for them, and re-layouts  2.09 us

profile of v4, /device:TPU:0, one launch (start us, length us, event | category | flops | bytes accessed | tf_op | source)
XLA Modules:
  0.0 44.1 jit_solution(4663149473378587907)
XLA Ops:
  0.6 41.4 %shard_map.95 = (f32[5,2048]{1,0:T(8,128)}, f32[4,1024]{1,0:T(4,128)}) custom-call(f32[4,4096]{1,0:T(4,128)} %attitude_ref.1, f32[5,4096]{1,0:T(8,128)} %design_ref.1, f32[1,4096]{1,0:T(1,128)} %bitcast.6, f32[1,4096]{1,0:T(1,128)} %bitcast.7, f32[1,4096]{1,0:T(1,128)} %bitcast.8, s32[1,4096]{1,0:T(1,128)} %bitcast.9, s32[1,4096]{1,0:T(1,128)} %bitcast.10, ...), custom_call_target="tpu_custom_call" | custom-call | tf_op jit(solution)/shard_map/pallas_call | solution.py:408
  42.0 0.0 copy-start
  42.0 1.5 %copy.12 = f32[5,2048]{1,0:T(8,128)} copy(f32[5,2048]{1,0:T(8,128)} %get-tuple-element.4) | data formatting | bytes 81920
  43.5 0.0 copy-done
  43.5 0.6 %copy.13 = f32[4,1024]{1,0:T(4,128)} copy(f32[4,1024]{1,0:T(4,128)S(1)} %copy-done) | data formatting | bytes 32768
Async XLA Ops:
  42.0 1.5 %copy-start = (f32[4,1024]{1,0:T(4,128)S(1)}, f32[4,1024]{1,0:T(4,128)}, u32[]{:S(2)}) copy-start(f32[4,1024]{1,0:T(4,128)} %get-tuple-element.5) | copy-start | bytes 49156
